TPU v7x, 32 devices: a whole 2x2x4 slice. The times are simulated.
32 devices in a mesh: dp: 16 (over z, y, x), tensor: 2 (over core).
Axes of the slice: x: 2, y: 2, z: 4, core: 2. Of those that a mesh axis runs over, the one named last changes fastest.
Arguments:
- tokens: bfloat16 [8192, 1024], P(('dp', 'tensor')), may hold values from -12 to 12
- enc_states: bfloat16 [4096, 1024], P(('dp', 'tensor')), may hold values from -12 to 12
- utt_lengths: int32 [16], P('dp'), may hold values from 256 to 512, as said below
- enc_lengths: int32 [16], P('dp'), may hold values from 128 to 256, as said below
- self_qkv: bfloat16 [3, 1024, 1024], P(None, 'dp', 'tensor'), may hold values from -0.1875 to 0.1875
- self_out: bfloat16 [1024, 1024], P('dp', 'tensor'), may hold values from -2 to 2
- cross_qkv: bfloat16 [3, 1024, 1024], P(None, 'dp', 'tensor'), may hold values from -0.1875 to 0.1875
- cross_out: bfloat16 [1024, 1024], P('dp', 'tensor'), may hold values from -1.5 to 1.5
- ffn_proj: bfloat16 [2, 1024, 4096], P(None, 'dp', 'tensor'), may hold values from -0.1875 to 0.1875
- norm_gains: bfloat16 [4, 1024], P(None, 'dp'), may hold values from 0.25 to 1.75
- norm_biases: bfloat16 [4, 1024], P(None, 'dp'), may hold values from -1.25 to 1.25
- cotangent: bfloat16 [8192, 1024], P(('dp', 'tensor')), may hold values from -12 to 12
Outputs:
- output: bfloat16 [8192, 1024], P(('dp', 'tensor'))
- token_grad: float32 [8192, 1024], P(('dp', 'tensor'))
- enc_grad: float32 [4096, 1024], P(('dp', 'tensor'))
- self_qkv_grad: float32 [3, 1024, 1024], P(None, 'dp', 'tensor')
- self_out_grad: float32 [1024, 1024], P('dp', 'tensor')
- cross_qkv_grad: float32 [3, 1024, 1024], P(None, 'dp', 'tensor')
- cross_out_grad: float32 [1024, 1024], P('dp', 'tensor')
- ffn_grad: float32 [2, 1024, 4096], P(None, 'dp', 'tensor')
- gains_grad: float32 [4, 1024], P(None, ('dp', 'tensor'))
- biases_grad: float32 [4, 1024], P(None, ('dp', 'tensor'))
Inputs may be any that keep to these rules, and one draw needn't show every extreme that they name: `utt_lengths`: valid unit tokens of each utterance; at least one utterance fills all 512 slots. `enc_lengths`: valid encoder states of each utterance; at least one utterance fills all 256 slots.
All inputs are finite; a program needn't handle non-finite values.
Results may differ from a plain program's by a relative error of at most 0.035.
Values may be sent and summed in bfloat16 or wider, within the bound.
No kernel may reach another device: no remote copies, remote signals or barrier semaphores. Data moves between devices by JAX's collectives and lax.ppermute only.
A program may use at most 192 MiB of HBM per device.

v0:
```python
import functools

import jax
import jax.numpy as jnp
from jax import lax
from jax.experimental import pallas as pl
from jax.experimental.pallas import tpu as pltpu
from jax.sharding import PartitionSpec as P

HEAD_DIM = 64
EPSILON = 1e-05
NEG_FILL = -1000000000.0
BF = jnp.bfloat16
F32 = jnp.float32


def dot(a, b, dims):
    return lax.dot_general(a, b, (dims, ((), ())), preferred_element_type=F32)


def mm(a, b):
    return dot(a, b, ((1,), (0,)))


def mm_t(a, b):
    return dot(a, b, ((1,), (1,)))


def t_mm(a, b):
    return dot(a, b, ((0,), (0,)))


def swap(values):
    return lax.ppermute(values, "tensor", [(0, 1), (1, 0)])


def normalize(values):
    centre = jnp.mean(values, axis=-1, keepdims=True)
    centred = values - centre
    spread = jnp.mean(centred * centred, axis=-1, keepdims=True)
    rstd = lax.rsqrt(spread + EPSILON)
    return centred * rstd, rstd


def gelu_both(z):
    c = 0.7978845608028654
    t = jnp.tanh(c * (z + 0.044715 * z * z * z))
    value = 0.5 * z * (1.0 + t)
    slope = 0.5 * (1.0 + t) + 0.5 * z * (1.0 - t * t) * c * (1.0 + 3.0 * 0.044715 * z * z)
    return value, slope


def masked(values, head):
    lane = lax.broadcasted_iota(jnp.int32, values.shape, 1)
    return jnp.where((lane < HEAD_DIM) == (head == 0), values, jnp.zeros_like(values))


def scores_of(keys, queries, start, limit, causal):
    raw = mm_t(keys, queries)
    key = lax.broadcasted_iota(jnp.int32, raw.shape, 0)
    allowed = key < limit
    if causal:
        query = start + lax.broadcasted_iota(jnp.int32, raw.shape, 1)
        allowed = allowed & (key <= query)
    return jnp.where(allowed, raw, NEG_FILL)


def blocks_of(rows, count, causal):
    if causal:
        half = rows // 2
        return [(0, half, half), (half, half, count)]
    return [(0, rows, count)]


def forward_kernel(causal, limit_ref, q_ref, k_ref, v_ref, out_ref, log_ref):
    limit = limit_ref[0]
    scale = HEAD_DIM ** (-0.5)
    for start, size, reach in blocks_of(q_ref.shape[0], k_ref.shape[0], causal):
        queries = (q_ref[start : start + size, :].astype(F32) * scale).astype(BF)
        mixed = None
        for head in range(2):
            keys = masked(k_ref[:reach, :], head)
            values = masked(v_ref[:reach, :], head)
            scores = scores_of(keys, queries, start, limit, causal)
            top = jnp.max(scores, axis=0, keepdims=True)
            exps = jnp.exp(scores - top)
            total = jnp.sum(exps, axis=0, keepdims=True)
            probs = (exps * (1.0 / total)).astype(BF)
            part = t_mm(probs, values)
            mixed = part if mixed is None else mixed + part
            log_ref[0, head : head + 1, start : start + size] = top + jnp.log(total)
        out_ref[start : start + size, :] = mixed.astype(BF)


def backward_kernel(
    causal, limit_ref, q_ref, k_ref, v_ref, do_ref, log_ref, dq_ref, dk_ref, dv_ref, sk, sv
):
    limit = limit_ref[0]
    scale = HEAD_DIM ** (-0.5)
    sk[...] = jnp.zeros_like(sk)
    sv[...] = jnp.zeros_like(sv)
    for start, size, reach in blocks_of(q_ref.shape[0], k_ref.shape[0], causal):
        queries = (q_ref[start : start + size, :].astype(F32) * scale).astype(BF)
        grad = do_ref[start : start + size, :]
        total = None
        for head in range(2):
            keys = masked(k_ref[:reach, :], head)
            values = masked(v_ref[:reach, :], head)
            scores = scores_of(keys, queries, start, limit, causal)
            probs = jnp.exp(scores - log_ref[0, head : head + 1, start : start + size])
            sv[:reach, :] += mm(probs.astype(BF), masked(grad, head))
            dprobs = mm_t(values, grad)
            inner = jnp.sum(dprobs * probs, axis=0, keepdims=True)
            ds = (probs * (dprobs - inner)).astype(BF)
            sk[:reach, :] += mm(ds, masked(queries, head))
            part = t_mm(ds, keys)
            total = part if total is None else total + part
        dq_ref[start : start + size, :] = (total * scale).astype(BF)
    dk_ref[...] = sk[...].astype(BF)
    dv_ref[...] = sv[...].astype(BF)


VMEM_LIMIT = 16 * 1024 * 1024


def params_of():
    return pltpu.CompilerParams(
        dimension_semantics=("arbitrary",), vmem_limit_bytes=VMEM_LIMIT
    )


def column_spec(rows, offset):
    return pl.BlockSpec((rows, 2 * HEAD_DIM), lambda i: (0, i + offset))


def log_spec(rows):
    return pl.BlockSpec((1, 2, rows), lambda i: (i, 0, 0))


SCALAR = pl.BlockSpec(memory_space=pltpu.SMEM)


def attend(limit, q, k, v, cols, causal):
    pairs = cols // (2 * HEAD_DIM)
    rows, count = q[0].shape[0], k[0].shape[0]
    work = rows * count * cols
    return pl.pallas_call(
        functools.partial(forward_kernel, causal),
        grid=(pairs,),
        in_specs=[SCALAR]
        + [column_spec(a.shape[0], at * pairs // cols) for a, at in (q, k, v)],
        out_specs=[column_spec(rows, 0), log_spec(rows)],
        out_shape=[
            jax.ShapeDtypeStruct((rows, cols), BF),
            jax.ShapeDtypeStruct((pairs, 2, rows), F32),
        ],
        compiler_params=params_of(),
        cost_estimate=pl.CostEstimate(
            flops=4 * work, bytes_accessed=8 * rows * cols, transcendentals=work // HEAD_DIM
        ),
    )(limit, q[0], k[0], v[0])


def attend_back(limit, q, k, v, grad, logs, cols, causal):
    pairs = cols // (2 * HEAD_DIM)
    rows, count = q[0].shape[0], k[0].shape[0]
    work = rows * count * cols
    return pl.pallas_call(
        functools.partial(backward_kernel, causal),
        grid=(pairs,),
        in_specs=[SCALAR]
        + [column_spec(a.shape[0], at * pairs // cols) for a, at in (q, k, v)]
        + [column_spec(rows, 0), log_spec(rows)],
        out_specs=[column_spec(rows, 0), column_spec(count, 0), column_spec(count, 0)],
        out_shape=[jax.ShapeDtypeStruct((n, cols), BF) for n in (rows, count, count)],
        scratch_shapes=[pltpu.VMEM((count, 2 * HEAD_DIM), F32) for i in range(2)],
        compiler_params=params_of(),
        cost_estimate=pl.CostEstimate(
            flops=10 * work, bytes_accessed=16 * rows * cols, transcendentals=work // HEAD_DIM
        ),
    )(limit, q[0], k[0], v[0], grad, logs)


def row_spec(rows, cols):
    return pl.BlockSpec((rows, cols), lambda i: (i, 0))


def fixed_spec(*shape):
    return pl.BlockSpec(shape, lambda i: (0,) * len(shape))


CHUNK = 16


def fold(values):
    return values[: CHUNK // 2] + values[CHUNK // 2 :]


def chunked(step, visit, width, sum_ref=None):
    zero = jnp.zeros((CHUNK // 2, width), F32)
    gain, shift = zero, zero
    for start in range(0, step, CHUNK):
        terms = visit(slice(start, start + CHUNK))
        if sum_ref is not None:
            gain, shift = gain + fold(terms[0]), shift + fold(terms[1])
    if sum_ref is None:
        return
    sums = jnp.concatenate(
        [jnp.sum(gain, axis=0, keepdims=True), jnp.sum(shift, axis=0, keepdims=True)]
    )
    first = pl.program_id(0) == 0

    @pl.when(first)
    def _():
        sum_ref[...] = sums

    @pl.when(jnp.logical_not(first))
    def _():
        sum_ref[...] += sums


def norm_grad(hat, rstd, gain, grad):
    scaled = grad * gain
    first = jnp.mean(scaled, axis=-1, keepdims=True)
    second = jnp.mean(scaled * hat, axis=-1, keepdims=True)
    return rstd * (scaled - first - hat * second)


def norm_kernel(index, x_ref, own_ref, other_ref, p_ref, new_ref, out_ref):
    step, width = x_ref.shape
    gain, shift = p_ref[index : index + 1, :], p_ref[index + 4 : index + 5, :]

    def visit(at):
        x = x_ref[at, :].astype(F32) + own_ref[at, :].astype(F32) + other_ref[at, :].astype(F32)
        new_ref[at, :] = x
        hat, rstd = normalize(x)
        out_ref[at, :] = (hat * gain + shift).astype(BF)

    chunked(step, visit, width)


def norm_rows(index, x, own, other, params):
    rows, width = x.shape
    step = rows // 4
    row = row_spec(step, width)
    return pl.pallas_call(
        functools.partial(norm_kernel, index),
        grid=(4,),
        in_specs=[row, row, row, fixed_spec(*params.shape)],
        out_specs=[row, row],
        out_shape=[
            jax.ShapeDtypeStruct((rows, width), F32),
            jax.ShapeDtypeStruct((rows, width), BF),
        ],
        compiler_params=params_of(),
        cost_estimate=pl.CostEstimate(
            flops=20 * rows * width, bytes_accessed=14 * rows * width, transcendentals=rows
        ),
    )(x, own, other, params)


def last_kernel(
    limit_ref, x_ref, own_ref, other_ref, p_ref, cot_ref, out_ref, dx_ref, dy_ref, sum_ref
):
    step, width = x_ref.shape
    gain, shift = p_ref[3:4, :], p_ref[7:8, :]
    begin = pl.program_id(0) * step

    def visit(at):
        x = x_ref[at, :] + own_ref[at, :].astype(F32) + other_ref[at, :].astype(F32)
        hat, rstd = normalize(x)
        out_ref[at, :] = (hat * gain + shift).astype(BF)
        row = begin + at.start + lax.broadcasted_iota(jnp.int32, (CHUNK, 1), 0)
        grad = cot_ref[at, :].astype(F32) * (row < limit_ref[0]).astype(F32)
        dx = norm_grad(hat, rstd, gain, grad)
        dx_ref[at, :] = dx
        dy_ref[at, :] = dx.astype(BF)
        return grad * hat, grad

    chunked(step, visit, width, sum_ref)


def norm_last(limit, x, own, other, params, cot):
    rows, width = x.shape
    step = rows // 4
    row = row_spec(step, width)
    return pl.pallas_call(
        last_kernel,
        grid=(4,),
        in_specs=[SCALAR, row, row, row, fixed_spec(*params.shape), row],
        out_specs=[row, row, row, fixed_spec(2, width)],
        out_shape=[
            jax.ShapeDtypeStruct((rows, width), BF),
            jax.ShapeDtypeStruct((rows, width), F32),
            jax.ShapeDtypeStruct((rows, width), BF),
            jax.ShapeDtypeStruct((2, width), F32),
        ],
        compiler_params=params_of(),
        cost_estimate=pl.CostEstimate(
            flops=40 * rows * width, bytes_accessed=20 * rows * width, transcendentals=rows
        ),
    )(limit, x, own, other, params, cot)


def back_kernel(index, x_ref, own_ref, other_ref, dres_ref, p_ref, dx_ref, *refs):
    step, width = x_ref.shape
    gain = p_ref[index : index + 1, :]

    def visit(at):
        hat, rstd = normalize(x_ref[at, :].astype(F32))
        grad = own_ref[at, :].astype(F32) + other_ref[at, :].astype(F32)
        dx = dres_ref[at, :] + norm_grad(hat, rstd, gain, grad)
        dx_ref[at, :] = dx
        if index:
            refs[0][at, :] = dx.astype(BF)
        return grad * hat, grad

    chunked(step, visit, width, refs[-1])


def norm_rows_back(index, x, own, other, dres, params):
    rows, width = x.shape
    step = rows // 4
    row = row_spec(step, width)
    lower = 1 if index else 0
    return pl.pallas_call(
        functools.partial(back_kernel, index),
        grid=(4,),
        in_specs=[row, row, row, row, fixed_spec(*params.shape)],
        out_specs=[row] + [row] * lower + [fixed_spec(2, width)],
        out_shape=[jax.ShapeDtypeStruct((rows, width), F32)]
        + [jax.ShapeDtypeStruct((rows, width), BF)] * lower
        + [jax.ShapeDtypeStruct((2, width), F32)],
        compiler_params=params_of(),
        cost_estimate=pl.CostEstimate(
            flops=30 * rows * width, bytes_accessed=18 * rows * width, transcendentals=rows
        ),
    )(x, own, other, dres, params)


FFN_STEPS = 4


def place_kernel(place_ref, from_ref, up_ref, down_ref, sems):
    blocks = place_ref.shape[0]
    size = up_ref.shape[0] // blocks
    copies = []
    for half, to_ref in enumerate((up_ref, down_ref)):
        for label in range(blocks):
            at = pl.multiple_of(place_ref[label] * size, size)
            copy = pltpu.make_async_copy(
                from_ref.at[half, pl.ds(at, size), :],
                to_ref.at[pl.ds(label * size, size), :],
                sems.at[half, label],
            )
            copy.start()
            copies.append(copy)
    for copy in copies:
        copy.wait()


def placed_weights(place, ffn):
    parts, width, units = ffn.shape
    anywhere = pl.BlockSpec(memory_space=pl.ANY)
    return pl.pallas_call(
        place_kernel,
        in_specs=[SCALAR, anywhere],
        out_specs=[anywhere] * 2,
        out_shape=[jax.ShapeDtypeStruct((width, units), BF)] * 2,
        scratch_shapes=[pltpu.SemaphoreType.DMA((2, place.shape[0]))],
        compiler_params=pltpu.CompilerParams(vmem_limit_bytes=1024 * 1024),
        cost_estimate=pl.CostEstimate(
            flops=0, bytes_accessed=4 * parts * width * units, transcendentals=0
        ),
    )(place, ffn)


def outer_kernel(place_ref, x_ref, d_ref, out_ref, turned):
    @pl.when(pl.program_id(0) == 0)
    def _():
        turned[...] = x_ref[...].T

    full = mm(turned[...], d_ref[...]).astype(BF)
    blocks = place_ref.shape[0]
    size = full.shape[0] // blocks
    for label in range(blocks):
        at = pl.multiple_of(place_ref[label] * size, size)
        out_ref[pl.ds(at, size), :] = full[label * size : (label + 1) * size]


def outer(place, x, d):
    rows, width = x.shape
    units = d.shape[1]
    step = units // FFN_STEPS
    col = pl.BlockSpec((width, step), lambda i: (0, i))
    return pl.pallas_call(
        outer_kernel,
        grid=(FFN_STEPS,),
        in_specs=[SCALAR, fixed_spec(rows, width), pl.BlockSpec((rows, step), lambda i: (0, i))],
        out_specs=col,
        out_shape=jax.ShapeDtypeStruct((width, units), BF),
        scratch_shapes=[pltpu.VMEM((width, rows), BF)],
        compiler_params=params_of(),
        cost_estimate=pl.CostEstimate(
            flops=2 * rows * width * units,
            bytes_accessed=2 * width * units + 2 * rows * units,
            transcendentals=0,
        ),
    )(place, x, d)


def terms_kernel(order, lines, *refs):
    step = pl.program_id(0)
    count, blocks = len(set(order)), len(order)
    lefts, rights, refs = refs[:count], refs[count : count + blocks], refs[count + blocks :]
    turned = refs[-count:]
    for block in range(blocks):

        @pl.when(step == block)
        def _(block=block):
            at = order[block]
            if order.index(at) == block:
                turned[at][...] = lefts[at][...].T
            full = mm(turned[at][...], rights[block][...]).astype(BF)
            quarter = full.shape[0] // 4
            if lines:
                keep_ref, send_ref = refs[:2]
                half = quarter // 2
                for label in range(4):
                    middle = label * quarter + half
                    keep_ref[0, label] = full[middle - half : middle]
                    send_ref[0, label] = full[middle : middle + half]
            else:
                one_ref, two_ref, y_ref, x_ref, own_ref = refs[:5]
                own_ref[0] = full[:quarter]
                y_ref[0] = full[quarter : 2 * quarter]
                x_ref[0] = full[2 * quarter : 3 * quarter]
                (one_ref if block < blocks // 2 else two_ref)[0] = full[3 * quarter :]


def grad_terms(lefts, order, rights, lines=False):
    width, cols = lefts[0].shape[1], rights[0].shape[1]
    blocks = len(order)
    middle = blocks // 2
    quarter = width // 4
    same = lambda i: i
    if lines:
        spec = pl.BlockSpec((1, 4, quarter // 2, cols), lambda i: (i, 0, 0, 0))
        out_specs = [spec] * 2
        out_shape = [jax.ShapeDtypeStruct((blocks, 4, quarter // 2, cols), BF)] * 2
    else:
        piece = lambda place: pl.BlockSpec((1, quarter, cols), lambda i: (place(i), 0, 0))
        shape = lambda n: jax.ShapeDtypeStruct((n, quarter, cols), BF)
        out_specs = [
            piece(lambda i: jnp.minimum(i, middle - 1)),
            piece(lambda i: jnp.maximum(i - middle, 0)),
        ] + [piece(same)] * 3
        out_shape = [shape(middle)] * 2 + [shape(blocks)] * 3
    return pl.pallas_call(
        functools.partial(terms_kernel, order, lines),
        grid=(blocks,),
        in_specs=[fixed_spec(*v.shape) for v in (*lefts, *rights)],
        out_specs=out_specs,
        out_shape=out_shape,
        scratch_shapes=[pltpu.VMEM((width, v.shape[0]), BF) for v in lefts],
        compiler_params=params_of(),
        cost_estimate=pl.CostEstimate(
            flops=2 * blocks * lefts[0].shape[0] * width * cols,
            bytes_accessed=2 * blocks * width * cols + 16 * lefts[0].shape[0] * width,
            transcendentals=0,
        ),
    )(*lefts, *rights)


def behind(values, earlier):
    return lax.optimization_barrier((values, earlier))[0]


def make_body(n_dp):
    bits = n_dp.bit_length() - 1
    assert n_dp == 1 << bits

    def hop(values, bit):
        return lax.ppermute(values, "dp", [(i, i ^ (1 << bit)) for i in range(n_dp)])

    far = range(bits - 1, 1, -1)

    def gather_far(held, bits_now, after):
        for bit in bits_now:
            after = hop(behind(held, after), bit)
            held = jnp.stack([held, after])
        return held, after

    def inner_rows(v, start, stop):
        return lax.slice_in_dim(v, start, stop, axis=v.ndim - 2)

    def gather_sides(held, after):
        held = behind(held, after)
        return hop(held, 0), hop(held, 1)

    def gather_corner(by_x, by_y, cut, after):
        first = behind(inner_rows(by_y, 0, cut), after)
        second = behind(inner_rows(by_x, cut, by_x.shape[-2]), after)
        return hop(first, 0), hop(second, 1)

    def gathered(held, sides, corner, cut):
        (by_x, by_y), (first, second) = sides, corner

        def rows(start, stop):
            last, offset = (first, 0) if stop <= cut else (second, cut)
            parts = [inner_rows(v, start, stop) for v in (held, by_y, by_x)]
            parts.append(inner_rows(last, start - offset, stop - offset))
            return jnp.concatenate(
                [v.reshape(-1, stop - start, v.shape[-1]) for v in parts]
            )

        return rows

    def full_weight(rows, start, stop):
        return rows(start, stop).reshape(-1, rows(start, stop).shape[-1])

    def plus(v, w):
        return (v.astype(F32) + w.astype(F32)).astype(BF)

    def scatter_near(pieces, late):
        one, two, for_y, for_x, own = pieces
        middle = one.shape[0]
        got_one, got_two = behind((hop(one, 0), hop(two, 1)), late)
        for_y = for_y.at[:middle].set(plus(for_y[:middle], got_one))
        for_x = for_x.at[middle:].set(plus(for_x[middle:], got_two))
        got_x, got_y = hop(for_x, 0), hop(for_y, 1)
        return own, (for_x, for_y), (got_x, got_y)

    def near_total(own, got):
        return own.astype(F32) + got[0].astype(F32) + got[1].astype(F32)

    def scatter_far(held):
        parts, feats, cols = held.shape
        held = held.reshape(parts, -1, feats * 4 // n_dp, cols)
        for count, bit in enumerate(reversed(far)):
            middle = held.shape[1] // 2
            held = held[:, :middle].astype(F32) + hop(held[:, middle:], bit).astype(F32)
            if count < len(far) - 1:
                held = held.astype(BF)
        return held[:, 0]

    def lines_first(keep, send):
        for count, bit in enumerate(reversed(far)):
            if count:
                middle = keep.shape[2] // 2
                keep, send = keep[:, :, :middle], keep[:, :, middle:]
            keep = plus(keep, hop(send, bit))
        middle = keep.shape[0] // 2
        return keep[:middle, 3], keep[middle:, 3], keep[:, 1], keep[:, 2], keep[:, 0]

    planes = [[4 * z + p for p in range(4)] for z in range(n_dp // 4)]
    lines = [[4 * z + p for z in range(n_dp // 4)] for p in range(4)]
    plane_first = [chip for line in lines for chip in line]

    def sum_plane(full):
        return lax.psum_scatter(
            full, "dp", scatter_dimension=0, tiled=True, axis_index_groups=planes
        )

    def sum_lines(full):
        return lax.psum_scatter(
            full, "dp", scatter_dimension=0, tiled=True, axis_index_groups=lines
        )

    def line_hops(full):
        rows, cols = full.shape
        held = full.reshape((2,) * len(far) + (rows * 4 // n_dp, cols))
        for count, bit in enumerate(reversed(far)):
            mine = (lax.axis_index("dp") >> bit) & 1
            axis = held.ndim - 3
            keep = lax.dynamic_index_in_dim(held, mine, axis, keepdims=False)
            send = lax.dynamic_index_in_dim(held, 1 - mine, axis, keepdims=False)
            held = keep.astype(F32) + hop(send.astype(BF), bit).astype(F32)
        return held

    def scatter_small(full, late):
        lead, feats = full.shape
        held = full.reshape((lead,) + (2,) * bits + (feats // n_dp,))
        for bit in reversed(far):
            keep = lax.index_in_dim(held, 0, 3, keepdims=False)
            held = keep + hop(lax.index_in_dim(held, 1, 3, keepdims=False), bit)
        held = behind(held, late)
        for bit in (0, 1):
            keep = lax.index_in_dim(held, 0, 1, keepdims=False)
            held = keep + hop(lax.index_in_dim(held, 1, 1, keepdims=False), bit)
        return held

    def body(
        tokens,
        enc_states,
        utt_lengths,
        enc_lengths,
        self_qkv,
        self_out,
        cross_qkv,
        cross_out,
        ffn_proj,
        norm_gains,
        norm_biases,
        cotangent,
    ):
        width = tokens.shape[1]
        feats = norm_gains.shape[1]
        core = lax.axis_index("tensor")
        me = lax.axis_index("dp")

        block = width // n_dp
        cols = jnp.arange(width, dtype=jnp.int32)
        labels = cols // block
        reverse = jnp.zeros_like(labels)
        for bit in range(bits):
            reverse = reverse | (((labels >> (bits - 1 - bit)) & 1) << bit)
        source = (me ^ reverse) * block + cols % block
        relabel = (cols[:, None] == source[None, :]).astype(BF)
        chip = source // block
        placed = ((chip & 3) * (n_dp // 4) + (chip >> 2)) * block + cols % block
        place = placed[::block] // block
        replace = (placed[:, None] == cols[None, :]).astype(BF)
        direct = feats % 16 == 0

        beside = lambda *v: jnp.concatenate(v, axis=-1)
        above = lambda *v: jnp.concatenate(v)
        params = jnp.concatenate([norm_gains, norm_biases]).reshape(1, 8 * feats)
        params = jnp.pad(params, ((0, 7), (0, 2 * self_out.shape[1] - 8 * feats)))
        ffn = lax.all_gather(
            ffn_proj, "dp", axis=1, tiled=True, axis_index_groups=[plane_first]
        )
        if direct:
            up, down = placed_weights(place, ffn)
        else:
            up, down = [mm(replace, ffn[i]).astype(BF) for i in (0, 1)]
            place = jnp.zeros((1,), jnp.int32)
        s_a = above(beside(self_qkv[0], self_qkv[1]), beside(self_qkv[2], self_out), params)
        s_c = above(beside(cross_qkv[1], cross_qkv[2]), beside(cross_qkv[0], cross_out))
        held_a, token = gather_far(s_a, far, norm_gains)
        sides_a = gather_sides(held_a, token)
        held_c, token = gather_far(s_c, far, token)
        corner_a = gather_corner(*sides_a, feats, sides_a)
        sides_c = gather_sides(held_c, sides_a)
        corner_c = gather_corner(*sides_c, feats, sides_c)
        weights = [
            gathered(held_a, sides_a, corner_a, feats),
            gathered(held_c, sides_c, corner_c, feats),
        ]
        w_qk, w_vo = full_weight(weights[0], 0, feats), full_weight(weights[0], feats, 2 * feats)
        params = weights[0](2 * feats, 2 * feats + 8)[:, 0, : 8 * feats]
        params = params.reshape(n_dp, 8, feats).transpose(1, 0, 2).reshape(8, width).astype(F32)
        c_kv, c_qo = [full_weight(weights[1], i * feats, (i + 1) * feats) for i in (0, 1)]
        inner_cols = self_out.shape[1]
        w_v, w_o = w_vo[:, :inner_cols], w_vo[:, inner_cols:]
        c_q, c_o = c_qo[:, :inner_cols], c_qo[:, inner_cols:]

        def whole(mine):
            other = swap(mine)
            return jnp.where(
                core == 0,
                jnp.concatenate([mine, other]),
                jnp.concatenate([other, mine]),
            )

        def relabeled(values):
            return mm(values, relabel).astype(BF)

        def own(values):
            size = values.shape[0] // 2
            return lax.dynamic_slice_in_dim(values, core * size, size)

        def other(values):
            size = values.shape[0] // 2
            return lax.dynamic_slice_in_dim(values, (1 - core) * size, size)

        def restored(values):
            high = values.astype(BF)
            low = (values - high.astype(F32)).astype(BF)
            return mm_t(high, relabel) + mm_t(low, relabel)

        x0 = whole(relabeled(tokens))
        enc = whole(relabeled(enc_states))
        cot = whole(relabeled(cotangent))

        hat0, rstd0 = normalize(x0.astype(F32))
        normed1 = (hat0 * params[0] + params[4]).astype(BF)
        qk1 = mm(normed1, w_qk).astype(BF)
        v1 = mm(normed1, w_v).astype(BF)
        first = (qk1, 0), (qk1, inner_cols), (v1, 0)
        o1, logs1 = attend(utt_lengths, *first, inner_cols, True)
        y1 = mm_t(o1, w_o).astype(BF)
        x1, normed2 = norm_rows(1, x0, y1, swap(y1), params)
        kv2 = mm(enc, c_kv).astype(BF)
        q2 = mm(normed2, c_q).astype(BF)
        second = (q2, 0), (kv2, 0), (kv2, inner_cols)
        q2, up, down = lax.optimization_barrier((q2, up, down))
        second = (q2, 0), (kv2, 0), (kv2, inner_cols)
        o2, logs2 = attend(enc_lengths, *second, inner_cols, False)
        y2 = mm_t(o2, c_o).astype(BF)
        x2, normed3 = norm_rows(2, x1, y2, swap(y2), params)
        act, slope = gelu_both(mm(normed3, up))
        act, slope = lax.optimization_barrier((act.astype(BF), slope.astype(BF)))
        y3 = mm_t(act, down).astype(BF)
        out, dx3, dy3, sums3 = norm_last(utt_lengths, x2, y3, swap(y3), params, cot)

        def for_planes(x, d):
            full = outer(place, x, d)
            return full if direct else t_mm(replace, full).astype(BF)

        d_down = for_planes(dy3, act)
        s_down = sum_plane(d_down)
        du = (mm(behind(dy3, d_down), down) * slope.astype(F32)).astype(BF)
        n3 = mm_t(du, up).astype(BF)
        s_up = sum_plane(for_planes(normed3, du))
        dx2, dy2, sums2 = norm_rows_back(2, x2, n3, swap(n3), dx3, params)
        do2 = mm(dy2, c_o).astype(BF)
        dq2, dk2, dv2 = attend_back(
            enc_lengths, *second, do2, logs2, inner_cols, False
        )
        terms_c = grad_terms((enc, normed2, dy2), (0, 0, 1, 2), (dk2, dv2, dq2, o2))
        n2 = mm_t(dq2, c_q).astype(BF)
        dx1, dy1, sums1 = norm_rows_back(1, x1, n2, swap(n2), dx2, params)
        do1 = mm(dy1, w_o).astype(BF)
        dq1, dk1, dv1 = attend_back(
            utt_lengths, *first, do1, logs1, inner_cols, True
        )
        own_c, sent_c, got_c = scatter_near(terms_c, do1)
        terms_qk = grad_terms((normed1,), (0, 0), (dq1, dk1))
        terms_vo = grad_terms((normed1, dy1), (0, 1), (dv1, o1), True)
        n1 = (mm_t(beside(dq1, dk1), w_qk) + mm_t(dv1, w_v)).astype(BF)
        dx0, sums0 = norm_rows_back(0, x0, n1, swap(n1), dx1, params)
        token_grad = restored(own(dx0))
        output = mm_t(own(out), relabel).astype(BF)
        enc_part = mm_t(dk2, c_kv[:, :inner_cols]) + mm_t(dv2, c_kv[:, inner_cols:])
        enc_grad = restored(own(enc_part) + swap(other(enc_part).astype(BF)).astype(F32))

        s_down = line_hops(s_down)
        own_qk, sent_qk, got_qk = scatter_near(terms_qk, dx0)
        s_up = sum_lines(behind(s_up, sent_qk))
        s_cross = scatter_far(near_total(own_c, got_c).astype(BF))
        s_vo, sent_vo, got_vo = scatter_near(lines_first(*terms_vo), sent_qk)
        s_vo = near_total(s_vo, got_vo)
        s_qk = scatter_far(near_total(own_qk, got_qk).astype(BF))
        sums = (sums0, sums1, sums2, sums3)
        terms = jnp.concatenate([v[:1] for v in sums] + [v[1:] for v in sums])
        terms = scatter_small(terms, got_qk)
        part = terms.shape[1] // 2
        terms = lax.dynamic_slice_in_dim(terms, core * part, part, axis=1)
        return (
            output,
            token_grad,
            enc_grad,
            jnp.concatenate([s_qk, s_vo[:1]]),
            s_vo[1],
            jnp.concatenate([s_cross[2:3], s_cross[:2]]),
            s_cross[3],
            jnp.stack([s_up.astype(F32), s_down]),
            terms[:4],
            terms[4:],
        )

    return body


def solution(mesh):
    return jax.shard_map(
        make_body(mesh.shape["dp"]),
        mesh=mesh,
        in_specs=(
            P(("dp", "tensor"), None),
            P(("dp", "tensor"), None),
            P("dp"),
            P("dp"),
            P(None, "dp", "tensor"),
            P("dp", "tensor"),
            P(None, "dp", "tensor"),
            P("dp", "tensor"),
            P(None, "dp", "tensor"),
            P(None, "dp"),
            P(None, "dp"),
            P(("dp", "tensor"), None),
        ),
        out_specs=(
            P(("dp", "tensor"), None),
            P(("dp", "tensor"), None),
            P(("dp", "tensor"), None),
            P(None, "dp", "tensor"),
            P("dp", "tensor"),
            P(None, "dp", "tensor"),
            P("dp", "tensor"),
            P(None, "dp", "tensor"),
            P(None, ("dp", "tensor")),
            P(None, ("dp", "tensor")),
        ),
        check_vma=False,
    )
```

profile of v0, /device:TPU:0, one launch (start us, length us, event | category | flops | bytes accessed | tf_op | source)
XLA Modules:
  0.0 424.6 jit_solution(13193740105961525227)
XLA Ops:
  10.6 4.1 collective-permute-start.1
  15.8 15.5 %collective-permute-done.1 = bf16[136,1024]{1,0:T(8,128)(2,1)S(1)} collective-permute-done((bf16[136,1024]{1,0:T(8,128)(2,1)S(1)}, bf16[136,1024]{1,0:T(8,128)(2,1)S(1)}, u32[]{:S(2)}, u32[]{:S(2)}) %collective-permute-start.1) | collective-permute-done | bytes 278560 | tf_op jit(solution)/shard_map/ppermute | solution.py:484
  31.4 4.6 %collective-permute-start.2 = (bf16[2,136,1024]{2,1,0:T(8,128)(2,1)S(1)}, bf16[2,136,1024]{2,1,0:T(8,128)(2,1)S(1)}, u32[]{:S(2)}, u32[]{:S(2)}) collective-permute-start(bf16[2,136,1024]{2,1,0:T(8,128)(2,1)S(1)} %get-tuple-element.147), channel_id=1, source_target_pairs={{0,8},{2,10},{4,12},{6,14},{8,0},{10,2},{12,4},{14,6},{16,24},{18,... | collective-permute-start | bytes 1671176 | tf_op jit(solution)/shard_map/ppermute | solution.py:484
  38.3 17.6 %collective-permute-done.2 = bf16[2,136,1024]{2,1,0:T(8,128)(2,1)S(1)} collective-permute-done((bf16[2,136,1024]{2,1,0:T(8,128)(2,1)S(1)}, bf16[2,136,1024]{2,1,0:T(8,128)(2,1)S(1)}, u32[]{:S(2)}, u32[]{:S(2)}) %collective-permute-start.2) | collective-permute-done | bytes 557088 | tf_op jit(solution)/shard_map/ppermute | solution.py:484
  59.8 3.7 collective-permute-start.8
  64.0 20.9 %collective-permute-done.8 = bf16[128,1024]{1,0:T(8,128)(2,1)S(1)} collective-permute-done((bf16[128,1024]{1,0:T(8,128)(2,1)S(1)}, bf16[128,1024]{1,0:T(8,128)(2,1)S(1)}, u32[]{:S(2)}, u32[]{:S(2)}) %collective-permute-start.8) | collective-permute-done | bytes 262176 | tf_op jit(solution)/shard_map/ppermute | solution.py:484
  90.7 27.8 %collective-permute-done.9 = bf16[2,128,1024]{2,1,0:T(8,128)(2,1)S(1)} collective-permute-done((bf16[2,128,1024]{2,1,0:T(8,128)(2,1)S(1)}, bf16[2,128,1024]{2,1,0:T(8,128)(2,1)S(1)}, u32[]{:S(2)}, u32[]{:S(2)}) %collective-permute-start.9) | collective-permute-done | bytes 524320 | tf_op jit(solution)/shard_map/ppermute | solution.py:484
  131.4 5.6 %shard_map.195 = (bf16[512,512]{1,0:T(8,128)(2,1)S(1)}, f32[4,2,512]{2,1,0:T(2,128)S(1)}) custom-call(s32[1]{0:T(128)S(6)} %copy.59.limit_ref, bf16[512,1024]{1,0:T(8,128)(2,1)S(1)} %convolution_convert_fusion.q_ref.k_ref, bf16[512,1024]{1,0:T(8,128)(2,1)S(1)} %convolution_convert_fusion.q_ref.k_ref, bf16[512,512]{1,0:T(8,128)(2,1)S(1)} %convolution_convert_fusion.10.v_ref), custom_call_target="tpu_custom_call" | custom-call | flops 536870912 | bytes 2097152 | tf_op jit(solution)/shard_map/pallas_call | solution.py:147
  137.9 15.5 %collective-permute-done.11 = bf16[2,2,128,1024]{3,2,1,0:T(8,128)(2,1)} collective-permute-done((bf16[2,2,128,1024]{3,2,1,0:T(8,128)(2,1)}, bf16[2,2,128,1024]{3,2,1,0:T(8,128)(2,1)}, u32[]{:S(2)}, u32[]{:S(2)}) %collective-permute-start.11) | collective-permute-done | bytes 1048608 | tf_op jit(solution)/shard_map/ppermute | solution.py:484
  163.5 5.0 %collective-permute-done.12 = bf16[2,2,64,1024]{3,2,1,0:T(8,128)(2,1)} collective-permute-done((bf16[2,2,64,1024]{3,2,1,0:T(8,128)(2,1)}, bf16[2,2,64,1024]{3,2,1,0:T(8,128)(2,1)}, u32[]{:S(2)}, u32[]{:S(2)}) %collective-permute-start.12) | collective-permute-done | bytes 524320 | tf_op jit(solution)/shard_map/ppermute | solution.py:484
  175.4 2.8 shard_map.196
  180.7 3.4 copy-done.4
  185.8 3.5 shard_map.198
  190.1 2.6 collective-permute-done.15.other_ref
  194.0 6.1 %fusion.5 = (bf16[512,2048]{1,0:T(8,128)(2,1)}, bf16[512,2048]{1,0:T(8,128)(2,1)S(1)}) fusion(bf16[512,1024]{1,0:T(8,128)(2,1)S(1)} %get-tuple-element.164.x_ref, bf16[1024,2048]{1,0:T(8,128)(2,1)S(1)} %get-tuple-element.165), kind=kOutput, calls=%fused_computation.7 | convolution fusion | flops 2168455168 | bytes 9437184 | tf_op jit(solution)/shard_map/dot_general | solution.py:18
  211.0 4.2 shard_map.201
  218.3 5.7 %multiply_convert_fusion.d_ref = bf16[512,2048]{1,0:T(8,128)(2,1)S(1)} fusion(bf16[512,2048]{1,0:T(8,128)(2,1)} %get-tuple-element.171, bf16[512,1024]{1,0:T(8,128)(2,1)} %copy-done.28, bf16[1024,2048]{1,0:T(8,128)(2,1)} %copy-done.23), kind=kOutput, calls=%fused_computation.8 | convolution fusion | flops 2150629376 | bytes 9437184 | tf_op jit(solution)/shard_map/dot_general | solution.py:18
  223.9 3.3 convolution_convert_fusion.4.own_ref
  230.2 4.2 shard_map.210
  236.6 3.0 fusion.31
  241.2 4.0 shard_map.202
  246.5 6.1 %shard_map.203 = (bf16[512,512]{1,0:T(8,128)(2,1)S(1)}, bf16[256,512]{1,0:T(8,128)(2,1)S(1)}, bf16[256,512]{1,0:T(8,128)(2,1)S(1)}) custom-call(s32[1]{0:T(128)S(6)} %copy.60.limit_ref, bf16[512,512]{1,0:T(8,128)(2,1)S(1)} %copy-done.34, bf16[256,1024]{1,0:T(8,128)(2,1)S(1)} %copy-done.32, bf16[256,1024]{1,0:T(8,128)(2,1)S(1)} %copy-done.32, ...), custom_call_target="tpu_custom_call" | custom-call | flops 671088640 | bytes 4194304 | tf_op jit(solution)/shard_map/pallas_call | solution.py:168
  256.7 3.7 shard_map.209
  268.1 8.2 %shard_map.205 = (bf16[512,512]{1,0:T(8,128)(2,1)S(1)}, bf16[512,512]{1,0:T(8,128)(2,1)S(1)}, bf16[512,512]{1,0:T(8,128)(2,1)S(1)}) custom-call(s32[1]{0:T(128)S(6)} %copy.59.limit_ref, bf16[512,1024]{1,0:T(8,128)(2,1)S(1)} %copy-done.38, bf16[512,1024]{1,0:T(8,128)(2,1)S(1)} %copy-done.38, bf16[512,512]{1,0:T(8,128)(2,1)S(1)} %copy-done.40, ...), custom_call_target="tpu_custom_call" | custom-call | flops 1342177280 | bytes 4194304 | tf_op jit(solution)/shard_map/pallas_call | solution.py:168
  290.8 13.5 %collective-permute-done.28 = bf16[2,4,128,512]{3,2,1,0:T(8,128)(2,1)S(1)} collective-permute-done((bf16[2,4,128,512]{3,2,1,0:T(8,128)(2,1)S(1)}, bf16[2,4,128,512]{3,2,1,0:T(8,128)(2,1)S(1)}, u32[]{:S(2)}, u32[]{:S(2)}) %collective-permute-start.28) | collective-permute-done | bytes 1048608 | tf_op jit(solution)/shard_map/ppermute | solution.py:484
  306.4 2.6 collective-permute-start.29
  316.8 3.2 fusion.28
  321.7 17.3 %collective-permute-done.37 = bf16[4,256,512]{2,1,0:T(8,128)(2,1)} collective-permute-done((bf16[4,256,512]{2,1,0:T(8,128)(2,1)}, bf16[4,256,512]{2,1,0:T(8,128)(2,1)}, u32[]{:S(2)}, u32[]{:S(2)}) %collective-permute-start.37) | collective-permute-done | bytes 1048608 | tf_op jit(solution)/shard_map/ppermute | solution.py:484
  340.5 2.5 add_convert_fusion
  346.5 9.8 %collective-permute-done.25 = bf16[2,256,512]{2,1,0:T(8,128)(2,1)} collective-permute-done((bf16[2,256,512]{2,1,0:T(8,128)(2,1)S(1)}, bf16[2,256,512]{2,1,0:T(8,128)(2,1)}, u32[]{:S(2)}, u32[]{:S(2)}) %collective-permute-start.25) | collective-permute-done | bytes 524320 | tf_op jit(solution)/shard_map/ppermute | solution.py:484
  378.6 28.9 %collective-permute-done.40 = bf16[2,64,2048]{2,1,0:T(8,128)(2,1)S(1)} collective-permute-done((bf16[2,64,2048]{2,1,0:T(8,128)(2,1)S(1)}, bf16[2,64,2048]{2,1,0:T(8,128)(2,1)S(1)}, u32[]{:S(2)}, u32[]{:S(2)}) %collective-permute-start.40) | collective-permute-done | bytes 524320 | tf_op jit(solution)/shard_map/ppermute | solution.py:484
  409.5 6.0 %collective-permute-done.41 = bf16[64,2048]{1,0:T(8,128)(2,1)S(1)} collective-permute-done((bf16[64,2048]{1,0:T(8,128)(2,1)S(1)}, bf16[64,2048]{1,0:T(8,128)(2,1)S(1)}, u32[]{:S(2)}, u32[]{:S(2)}) %collective-permute-start.41) | collective-permute-done | bytes 262176 | tf_op jit(solution)/shard_map/ppermute | solution.py:484
  (343 shorter events, 142.7 us)
Async XLA Ops:
  7.2 173.5 %all-gather.2.cloned.1.call-start = ((), (), s32[]{:S(2)}) async-start(), calls=%async_computation.3 | async-start | bytes 8912896 | tf_op jit(solution)/shard_map/all_gather | solution.py:630
  7.9 367.9 %reduce-scatter.8.cloned.1.call-start = ((), (), s32[]{:S(2)}) async-start(), calls=%async_computation.6 | async-start | bytes 5242880 | tf_op jit(solution)/shard_map/reduce_scatter | solution.py:561
  10.6 20.7 %collective-permute-start.1 = (bf16[136,1024]{1,0:T(8,128)(2,1)S(1)}, bf16[136,1024]{1,0:T(8,128)(2,1)S(1)}, u32[]{:S(2)}, u32[]{:S(2)}) collective-permute-start(bf16[136,1024]{1,0:T(8,128)(2,1)S(1)} %fusion.62), channel_id=1, source_target_pairs={{0,16},{2,18},{4,20},{6,22},{8,24},{10,26},{12,28},{14,30},{16,0},... | collective-permute-start | bytes 835592 | tf_op jit(solution)/shard_map/ppermute | solution.py:484
  15.7 42.2 %collective-permute-start = (bf16[256,1024]{1,0:T(8,128)(2,1)S(1)}, bf16[256,1024]{1,0:T(8,128)(2,1)S(1)}, u32[]{:S(2)}, u32[]{:S(2)}) collective-permute-start(bf16[256,1024]{1,0:T(8,128)(2,1)S(1)} %fusion.33), channel_id=1, source_target_pairs={{0,1},{1,0},{2,3},{3,2},{4,5},{5,4},{6,7},{7,6},{8,9},{9,8},{10,11... | collective-permute-start | bytes 1572872 | tf_op jit(solution)/shard_map/ppermute | solution.py:34
  31.4 24.5 %collective-permute-start.2 = (bf16[2,136,1024]{2,1,0:T(8,128)(2,1)S(1)}, bf16[2,136,1024]{2,1,0:T(8,128)(2,1)S(1)}, u32[]{:S(2)}, u32[]{:S(2)}) collective-permute-start(bf16[2,136,1024]{2,1,0:T(8,128)(2,1)S(1)} %get-tuple-element.147), channel_id=1, source_target_pairs={{0,8},{2,10},{4,12},{6,14},{8,0},{10,2},{12,4},{14,6},{16,24},{18,... | collective-permute-start | bytes 1671176 | tf_op jit(solution)/shard_map/ppermute | solution.py:484
  37.5 123.3 %collective-permute-start.13 = (bf16[128,1024]{1,0:T(8,128)(2,1)}, bf16[128,1024]{1,0:T(8,128)(2,1)}, u32[]{:S(2)}, u32[]{:S(2)}) collective-permute-start(bf16[128,1024]{1,0:T(8,128)(2,1)} %fusion.36), channel_id=1, source_target_pairs={{0,1},{1,0},{2,3},{3,2},{4,5},{5,4},{6,7},{7,6},{8,9},{9,8},{10,11... | collective-permute-start | bytes 786440 | tf_op jit(solution)/shard_map/ppermute | solution.py:34
  56.0 29.1 %collective-permute-start.3 = (bf16[2,2,136,1024]{3,2,1,0:T(8,128)(2,1)S(1)}, bf16[2,2,136,1024]{3,2,1,0:T(8,128)(2,1)S(1)}, u32[]{:S(2)}, u32[]{:S(2)}) collective-permute-start(bf16[2,2,136,1024]{3,2,1,0:T(8,128)(2,1)S(1)} %pad_maximum_fusion.4), channel_id=1, source_target_pairs={{0,4},{2,6},{4,0},{6,2},{8,12},{10,14},{12,8},{14,10},{16,20},{18,... | collective-permute-start | bytes 3342344 | tf_op jit(solution)/shard_map/ppermute | solution.py:484
  58.2 29.5 %collective-permute-start.4 = (bf16[2,2,136,1024]{3,2,1,0:T(8,128)(2,1)S(1)}, bf16[2,2,136,1024]{3,2,1,0:T(8,128)(2,1)S(1)}, u32[]{:S(2)}, u32[]{:S(2)}) collective-permute-start(bf16[2,2,136,1024]{3,2,1,0:T(8,128)(2,1)S(1)} %pad_maximum_fusion.4), channel_id=1, source_target_pairs={{0,2},{2,0},{4,6},{6,4},{8,10},{10,8},{12,14},{14,12},{16,18},{18,... | collective-permute-start | bytes 3342344 | tf_op jit(solution)/shard_map/ppermute | solution.py:484
  59.8 25.1 %collective-permute-start.8 = (bf16[128,1024]{1,0:T(8,128)(2,1)S(1)}, bf16[128,1024]{1,0:T(8,128)(2,1)S(1)}, u32[]{:S(2)}, u32[]{:S(2)}) collective-permute-start(bf16[128,1024]{1,0:T(8,128)(2,1)S(1)} %get-tuple-element.154), channel_id=1, source_target_pairs={{0,16},{2,18},{4,20},{6,22},{8,24},{10,26},{12,28},{14,30},{16,0},... | collective-permute-start | bytes 786440 | tf_op jit(solution)/shard_map/ppermute | solution.py:484
  85.0 33.6 %collective-permute-start.9 = (bf16[2,128,1024]{2,1,0:T(8,128)(2,1)S(1)}, bf16[2,128,1024]{2,1,0:T(8,128)(2,1)S(1)}, u32[]{:S(2)}, u32[]{:S(2)}) collective-permute-start(bf16[2,128,1024]{2,1,0:T(8,128)(2,1)S(1)} %get-tuple-element.155), channel_id=1, source_target_pairs={{0,8},{2,10},{4,12},{6,14},{8,0},{10,2},{12,4},{14,6},{16,24},{18,... | collective-permute-start | bytes 1572872 | tf_op jit(solution)/shard_map/ppermute | solution.py:484
  87.7 35.2 %collective-permute-start.6 = (bf16[2,2,64,1024]{3,2,1,0:T(8,128)(2,1)S(1)}, bf16[2,2,64,1024]{3,2,1,0:T(8,128)(2,1)S(1)}, u32[]{:S(2)}, u32[]{:S(2)}) collective-permute-start(bf16[2,2,64,1024]{3,2,1,0:T(8,128)(2,1)S(1)} %get-tuple-element.150), channel_id=1, source_target_pairs={{0,2},{2,0},{4,6},{6,4},{8,10},{10,8},{12,14},{14,12},{16,18},{18,... | collective-permute-start | bytes 1572872 | tf_op jit(solution)/shard_map/ppermute | solution.py:484
  88.9 35.6 %collective-permute-start.5 = (bf16[2,2,72,1024]{3,2,1,0:T(8,128)(2,1)S(1)}, bf16[2,2,72,1024]{3,2,1,0:T(8,128)(2,1)S(1)}, u32[]{:S(2)}, u32[]{:S(2)}) collective-permute-start(bf16[2,2,72,1024]{3,2,1,0:T(8,128)(2,1)S(1)} %slice.466), channel_id=1, source_target_pairs={{0,4},{2,6},{4,0},{6,2},{8,12},{10,14},{12,8},{14,10},{16,20},{18,... | collective-permute-start | bytes 1769480 | tf_op jit(solution)/shard_map/ppermute | solution.py:484
  119.7 33.7 %collective-permute-start.11 = (bf16[2,2,128,1024]{3,2,1,0:T(8,128)(2,1)}, bf16[2,2,128,1024]{3,2,1,0:T(8,128)(2,1)}, u32[]{:S(2)}, u32[]{:S(2)}) collective-permute-start(bf16[2,2,128,1024]{3,2,1,0:T(8,128)(2,1)} %pad_maximum_fusion.5), channel_id=1, source_target_pairs={{0,2},{2,0},{4,6},{6,4},{8,10},{10,8},{12,14},{14,12},{16,18},{18,... | collective-permute-start | bytes 3145736 | tf_op jit(solution)/shard_map/ppermute | solution.py:484
  121.1 34.8 %collective-permute-start.10 = (bf16[2,2,128,1024]{3,2,1,0:T(8,128)(2,1)}, bf16[2,2,128,1024]{3,2,1,0:T(8,128)(2,1)}, u32[]{:S(2)}, u32[]{:S(2)}) collective-permute-start(bf16[2,2,128,1024]{3,2,1,0:T(8,128)(2,1)} %pad_maximum_fusion.5), channel_id=1, source_target_pairs={{0,4},{2,6},{4,0},{6,2},{8,12},{10,14},{12,8},{14,10},{16,20},{18,... | collective-permute-start | bytes 3145736 | tf_op jit(solution)/shard_map/ppermute | solution.py:484
  137.8 37.1 %collective-permute-start.7 = (bf16[512,1024]{1,0:T(8,128)(2,1)S(1)}, bf16[512,1024]{1,0:T(8,128)(2,1)}, u32[]{:S(2)}, u32[]{:S(2)}) collective-permute-start(bf16[512,1024]{1,0:T(8,128)(2,1)S(1)} %convolution_convert_fusion.3.own_ref), channel_id=1, source_target_pairs={{0,1},{1,0},{2,3},{3,2},{4,5},{5,4},{6,7},{7,6},{8,9},{9,8},{10,11... | collective-permute-start | bytes 3145736 | tf_op jit(solution)/shard_map/ppermute | solution.py:34
  218.2 158.9 %reduce-scatter.4.cloned.1.call-start = ((), (), s32[]{:S(2)}) async-start(), calls=%async_computation.4 | async-start | bytes 5242880 | tf_op jit(solution)/shard_map/reduce_scatter | solution.py:561
  236.5 179.0 %reduce-scatter.6.cloned.1.call-start = ((), (), s32[]{:S(2)}) async-start(), calls=%async_computation.5 | async-start | bytes 1310720 | tf_op jit(solution)/shard_map/reduce_scatter | solution.py:566
  260.3 24.5 %collective-permute-start.34 = (bf16[2,256,512]{2,1,0:T(8,128)(2,1)S(1)}, bf16[2,256,512]{2,1,0:T(8,128)(2,1)S(1)}, u32[]{:S(2)}, u32[]{:S(2)}) collective-permute-start(bf16[2,256,512]{2,1,0:T(8,128)(2,1)S(1)} %get-tuple-element.199), channel_id=1, source_target_pairs={{0,2},{2,0},{4,6},{6,4},{8,10},{10,8},{12,14},{14,12},{16,18},{18,... | collective-permute-start | bytes 1572872 | tf_op jit(solution)/shard_map/ppermute | solution.py:484
  260.5 25.2 %collective-permute-start.35 = (bf16[2,256,512]{2,1,0:T(8,128)(2,1)S(1)}, bf16[2,256,512]{2,1,0:T(8,128)(2,1)S(1)}, u32[]{:S(2)}, u32[]{:S(2)}) collective-permute-start(bf16[2,256,512]{2,1,0:T(8,128)(2,1)S(1)} %get-tuple-element.200), channel_id=1, source_target_pairs={{0,4},{2,6},{4,0},{6,2},{8,12},{10,14},{12,8},{14,10},{16,20},{18,... | collective-permute-start | bytes 1572872 | tf_op jit(solution)/shard_map/ppermute | solution.py:484
  279.4 24.9 %collective-permute-start.28 = (bf16[2,4,128,512]{3,2,1,0:T(8,128)(2,1)S(1)}, bf16[2,4,128,512]{3,2,1,0:T(8,128)(2,1)S(1)}, u32[]{:S(2)}, u32[]{:S(2)}) collective-permute-start(bf16[2,4,128,512]{3,2,1,0:T(8,128)(2,1)S(1)} %get-tuple-element.194), channel_id=1, source_target_pairs={{0,8},{2,10},{4,12},{6,14},{8,0},{10,2},{12,4},{14,6},{16,24},{18,... | collective-permute-start | bytes 3145736 | tf_op jit(solution)/shard_map/ppermute | solution.py:484
  282.3 24.1 %collective-permute-start.20 = (bf16[512,1024]{1,0:T(8,128)(2,1)S(1)}, bf16[512,1024]{1,0:T(8,128)(2,1)S(1)}, u32[]{:S(2)}, u32[]{:S(2)}) collective-permute-start(bf16[512,1024]{1,0:T(8,128)(2,1)S(1)} %add_convert_fusion.2.own_ref), channel_id=1, source_target_pairs={{0,1},{1,0},{2,3},{3,2},{4,5},{5,4},{6,7},{7,6},{8,9},{9,8},{10,11... | collective-permute-start | bytes 3145736 | tf_op jit(solution)/shard_map/ppermute | solution.py:34
  283.9 28.5 %collective-permute-start.22 = (bf16[1,256,512]{2,1,0:T(8,128)(2,1)S(1)}, bf16[1,256,512]{2,1,0:T(8,128)(2,1)S(1)}, u32[]{:S(2)}, u32[]{:S(2)}) collective-permute-start(bf16[1,256,512]{2,1,0:T(8,128)(2,1)S(1)} %get-tuple-element.188), channel_id=1, source_target_pairs={{0,2},{2,0},{4,6},{6,4},{8,10},{10,8},{12,14},{14,12},{16,18},{18,... | collective-permute-start | bytes 786440 | tf_op jit(solution)/shard_map/ppermute | solution.py:484
  284.8 27.6 %collective-permute-start.23 = (bf16[1,256,512]{2,1,0:T(8,128)(2,1)S(1)}, bf16[1,256,512]{2,1,0:T(8,128)(2,1)S(1)}, u32[]{:S(2)}, u32[]{:S(2)}) collective-permute-start(bf16[1,256,512]{2,1,0:T(8,128)(2,1)S(1)} %get-tuple-element.189), channel_id=1, source_target_pairs={{0,4},{2,6},{4,0},{6,2},{8,12},{10,14},{12,8},{14,10},{16,20},{18,... | collective-permute-start | bytes 786440 | tf_op jit(solution)/shard_map/ppermute | solution.py:484
  287.7 51.2 %collective-permute-start.37 = (bf16[4,256,512]{2,1,0:T(8,128)(2,1)}, bf16[4,256,512]{2,1,0:T(8,128)(2,1)}, u32[]{:S(2)}, u32[]{:S(2)}) collective-permute-start(bf16[4,256,512]{2,1,0:T(8,128)(2,1)} %fusion.54), channel_id=1, source_target_pairs={{0,4},{2,6},{4,0},{6,2},{8,12},{10,14},{12,8},{14,10},{16,20},{18,... | collective-permute-start | bytes 3145736 | tf_op jit(solution)/shard_map/ppermute | solution.py:484
  304.3 36.2 %collective-permute-start.36 = (bf16[4,256,512]{2,1,0:T(8,128)(2,1)}, bf16[4,256,512]{2,1,0:T(8,128)(2,1)}, u32[]{:S(2)}, u32[]{:S(2)}) collective-permute-start(bf16[4,256,512]{2,1,0:T(8,128)(2,1)} %fusion.53), channel_id=1, source_target_pairs={{0,2},{2,0},{4,6},{6,4},{8,10},{10,8},{12,14},{14,12},{16,18},{18,... | collective-permute-start | bytes 3145736 | tf_op jit(solution)/shard_map/ppermute | solution.py:484
  306.4 38.1 %collective-permute-start.29 = (bf16[2,4,64,512]{3,2,1,0:T(8,128)(2,1)}, bf16[2,4,64,512]{3,2,1,0:T(8,128)(2,1)S(1)}, u32[]{:S(2)}, u32[]{:S(2)}) collective-permute-start(bf16[2,4,64,512]{3,2,1,0:T(8,128)(2,1)} %slice.498), channel_id=1, source_target_pairs={{0,16},{2,18},{4,20},{6,22},{8,24},{10,26},{12,28},{14,30},{16,0},... | collective-permute-start | bytes 1572872 | tf_op jit(solution)/shard_map/ppermute | solution.py:484
  312.5 43.9 %collective-permute-start.25 = (bf16[2,256,512]{2,1,0:T(8,128)(2,1)S(1)}, bf16[2,256,512]{2,1,0:T(8,128)(2,1)}, u32[]{:S(2)}, u32[]{:S(2)}) collective-permute-start(bf16[2,256,512]{2,1,0:T(8,128)(2,1)S(1)} %fusion.64), channel_id=1, source_target_pairs={{0,4},{2,6},{4,0},{6,2},{8,12},{10,14},{12,8},{14,10},{16,20},{18,... | collective-permute-start | bytes 1572872 | tf_op jit(solution)/shard_map/ppermute | solution.py:484
  320.1 36.2 %collective-permute-start.24 = (bf16[2,256,512]{2,1,0:T(8,128)(2,1)S(1)}, bf16[2,256,512]{2,1,0:T(8,128)(2,1)S(1)}, u32[]{:S(2)}, u32[]{:S(2)}) collective-permute-start(bf16[2,256,512]{2,1,0:T(8,128)(2,1)S(1)} %fusion.63), channel_id=1, source_target_pairs={{0,2},{2,0},{4,6},{6,4},{8,10},{10,8},{12,14},{14,12},{16,18},{18,... | collective-permute-start | bytes 1572872 | tf_op jit(solution)/shard_map/ppermute | solution.py:484
  343.1 18.7 %collective-permute-start.38 = (bf16[4,2,64,512]{3,2,1,0:T(8,128)(2,1)S(1)}, bf16[4,2,64,512]{3,2,1,0:T(8,128)(2,1)S(1)}, u32[]{:S(2)}, u32[]{:S(2)}) collective-permute-start(bf16[4,2,64,512]{3,2,1,0:T(8,128)(2,1)S(1)} %slice.509), channel_id=1, source_target_pairs={{0,8},{2,10},{4,12},{6,14},{8,0},{10,2},{12,4},{14,6},{16,24},{18,... | collective-permute-start | bytes 1572872 | tf_op jit(solution)/shard_map/ppermute | solution.py:484
  344.7 19.2 %collective-permute-start.30 = (bf16[1,64,512]{2,1,0:T(8,128)(2,1)S(1)}, bf16[1,64,512]{2,1,0:T(8,128)(2,1)S(1)}, u32[]{:S(2)}, u32[]{:S(2)}) collective-permute-start(bf16[1,64,512]{2,1,0:T(8,128)(2,1)S(1)} %get-tuple-element.239), channel_id=1, source_target_pairs={{0,2},{2,0},{4,6},{6,4},{8,10},{10,8},{12,14},{14,12},{16,18},{18,... | collective-permute-start | bytes 196616 | tf_op jit(solution)/shard_map/ppermute | solution.py:484
  372.0 35.7 %collective-permute-start.27 = (bf16[2,1,64,512]{3,2,0,1:T(8,128)(2,1)}, bf16[2,1,64,512]{3,2,0,1:T(8,128)(2,1)}, u32[]{:S(2)}, u32[]{:S(2)}) collective-permute-start(bf16[2,1,64,512]{3,2,0,1:T(8,128)(2,1)} %slice.496), channel_id=1, source_target_pairs={{0,16},{2,18},{4,20},{6,22},{8,24},{10,26},{12,28},{14,30},{16,0},... | collective-permute-start | bytes 393224 | tf_op jit(solution)/shard_map/ppermute | solution.py:484
  377.0 30.5 %collective-permute-start.40 = (bf16[2,64,2048]{2,1,0:T(8,128)(2,1)S(1)}, bf16[2,64,2048]{2,1,0:T(8,128)(2,1)S(1)}, u32[]{:S(2)}, u32[]{:S(2)}) collective-permute-start(bf16[2,64,2048]{2,1,0:T(8,128)(2,1)S(1)} %dynamic-slice_bitcast_fusion), channel_id=1, source_target_pairs={{0,8},{2,10},{4,12},{6,14},{8,0},{10,2},{12,4},{14,6},{16,24},{18,... | collective-permute-start | bytes 1572872 | tf_op jit(solution)/shard_map/ppermute | solution.py:484
  (83 other events, 529.9 us)
Sparse Core Ops, SparseCore 0:
  10.8 155.3 all-gather.1
  218.3 57.7 reduce-scatter.7
  279.4 84.0 reduce-scatter.3
  377.2 32.1 reduce-scatter.5
where the time goes:
time: 433 us; the launch traced here: 425 us
  waiting for transfers between devices  195 us (45%)
  Pallas kernels  54.7 us (13%)
  starting transfers between devices  50.1 us (12%)
  matrix products  43.9 us (10%)
  local copies, waits for them, and re-layouts  37.4 us (9%)
  other arithmetic  26.8 us (6%)
  between operations  16.9 us (4%)
    ppermute x36, waiting for transfers between devices, hop(): return lax.ppermute(values, 'dp', [(i, i ^ 1 << bit) for i in range(n_dp)])  189 us
    ppermute x36, starting transfers between devices, hop(): return lax.ppermute(values, 'dp', [(i, i ^ 1 << bit) for i in range(n_dp)])  48.1 us
    dot_general x25, matrix products, dot(): return lax.dot_general(a, b, (dims, ((), ())), preferred_element_type=F32)  43.9 us
    unnamed x132, local copies, waits for them, and re-layouts  23.9 us
    pallas_call x2, Pallas kernels, attend_back(): pl.pallas_call(functools.partial(backward_kernel, causal), grid=(pairs,),...  14.3 us
    pallas_call x2, Pallas kernels, attend(): pl.pallas_call(functools.partial(forward_kernel, causal), grid=(pairs,),...  9.11 us
  transfers between devices with their start and end apart: 50, of which 21 were waited for; matrix products, arithmetic and copies ran while one was open for 17% of the time, Pallas kernels for 10%

commit v1 on v0

--- a/solution.py
+++ b/solution.py
@@ -44,10 +44,11 @@
 
 def gelu_both(z):
     c = 0.7978845608028654
-    t = jnp.tanh(c * (z + 0.044715 * z * z * z))
-    value = 0.5 * z * (1.0 + t)
-    slope = 0.5 * (1.0 + t) + 0.5 * z * (1.0 - t * t) * c * (1.0 + 3.0 * 0.044715 * z * z)
-    return value, slope
+    square = z * z
+    t = jnp.tanh(z * (c + 0.044715 * c * square))
+    gate = 0.5 + 0.5 * t
+    value = z * gate
+    return value, gate + value * (1.0 - t) * (c + 3.0 * 0.044715 * c * square)
 
 
 def masked(values, head):
@@ -364,7 +365,7 @@
     anywhere = pl.BlockSpec(memory_space=pl.ANY)
     return pl.pallas_call(
         place_kernel,
-        in_specs=[SCALAR, anywhere],
+        in_specs=[SCALAR, pl.BlockSpec(memory_space=pltpu.HBM)],
         out_specs=[anywhere] * 2,
         out_shape=[jax.ShapeDtypeStruct((width, units), BF)] * 2,
         scratch_shapes=[pltpu.SemaphoreType.DMA((2, place.shape[0]))],
@@ -398,7 +399,7 @@
         grid=(FFN_STEPS,),
         in_specs=[SCALAR, fixed_spec(rows, width), pl.BlockSpec((rows, step), lambda i: (0, i))],
         out_specs=col,
-        out_shape=jax.ShapeDtypeStruct((width, units), BF),
+        out_shape=pltpu.HBM((width, units), BF),
         scratch_shapes=[pltpu.VMEM((width, rows), BF)],
         compiler_params=params_of(),
         cost_estimate=pl.CostEstimate(

time: 433 us -> 430 us (level)
    unnamed x132 -> x134, local copies, waits for them, and re-layouts: 23.9 us -> 21.2 us
  transfers between devices with their start and end apart: 50 -> 50, of which waited for: 21 -> 22; matrix products, arithmetic and copies ran while one was open for 17% -> 17% of each run, Pallas kernels for 10% -> 10%
where the time goes in v1:
time: 430 us; the launch traced here: 423 us
  waiting for transfers between devices  194 us (45%)
  Pallas kernels  57.2 us (13%)
  starting transfers between devices  49.5 us (12%)
  matrix products  39.9 us (9%)
  local copies, waits for them, and re-layouts  34.6 us (8%)
  other arithmetic  30.8 us (7%)
  between operations  16.9 us (4%)
    ppermute x36, waiting for transfers between devices, hop(): return lax.ppermute(values, 'dp', [(i, i ^ 1 << bit) for i in range(n_dp)])  188 us
    ppermute x36, starting transfers between devices, hop(): return lax.ppermute(values, 'dp', [(i, i ^ 1 << bit) for i in range(n_dp)])  47.8 us
    dot_general x25, matrix products, dot(): return lax.dot_general(a, b, (dims, ((), ())), preferred_element_type=F32)  39.9 us
    unnamed x134, local copies, waits for them, and re-layouts  21.2 us
    pallas_call x2, Pallas kernels, attend_back(): pl.pallas_call(functools.partial(backward_kernel, causal), grid=(pairs,),...  14.3 us
    pallas_call x2, Pallas kernels, outer(): pl.pallas_call(outer_kernel, grid=(FFN_STEPS,), in_specs=[SCALAR, fixed_s...  10.4 us
    pallas_call x2, Pallas kernels, attend(): pl.pallas_call(functools.partial(forward_kernel, causal), grid=(pairs,),...  9.1 us
  transfers between devices with their start and end apart: 50, of which 22 were waited for; matrix products, arithmetic and copies ran while one was open for 17% of the time, Pallas kernels for 10%

profile of v1, /device:TPU:0, one launch (start us, length us, event | category | flops | bytes accessed | tf_op | source)
XLA Modules:
  0.0 422.5 jit_solution(9352655060951599387)
XLA Ops:
  10.6 4.1 collective-permute-start.1
  15.8 15.5 %collective-permute-done.1 = bf16[136,1024]{1,0:T(8,128)(2,1)S(1)} collective-permute-done((bf16[136,1024]{1,0:T(8,128)(2,1)S(1)}, bf16[136,1024]{1,0:T(8,128)(2,1)S(1)}, u32[]{:S(2)}, u32[]{:S(2)}) %collective-permute-start.1) | collective-permute-done | bytes 278560 | tf_op jit(solution)/shard_map/ppermute | solution.py:485
  31.4 4.6 %collective-permute-start.2 = (bf16[2,136,1024]{2,1,0:T(8,128)(2,1)S(1)}, bf16[2,136,1024]{2,1,0:T(8,128)(2,1)S(1)}, u32[]{:S(2)}, u32[]{:S(2)}) collective-permute-start(bf16[2,136,1024]{2,1,0:T(8,128)(2,1)S(1)} %get-tuple-element.147), channel_id=1, source_target_pairs={{0,8},{2,10},{4,12},{6,14},{8,0},{10,2},{12,4},{14,6},{16,24},{18,... | collective-permute-start | bytes 1671176 | tf_op jit(solution)/shard_map/ppermute | solution.py:485
  37.7 18.2 %collective-permute-done.2 = bf16[2,136,1024]{2,1,0:T(8,128)(2,1)S(1)} collective-permute-done((bf16[2,136,1024]{2,1,0:T(8,128)(2,1)S(1)}, bf16[2,136,1024]{2,1,0:T(8,128)(2,1)S(1)}, u32[]{:S(2)}, u32[]{:S(2)}) %collective-permute-start.2) | collective-permute-done | bytes 557088 | tf_op jit(solution)/shard_map/ppermute | solution.py:485
  61.1 3.7 collective-permute-start.8
  65.2 20.0 %collective-permute-done.8 = bf16[128,1024]{1,0:T(8,128)(2,1)S(1)} collective-permute-done((bf16[128,1024]{1,0:T(8,128)(2,1)S(1)}, bf16[128,1024]{1,0:T(8,128)(2,1)S(1)}, u32[]{:S(2)}, u32[]{:S(2)}) %collective-permute-start.8) | collective-permute-done | bytes 262176 | tf_op jit(solution)/shard_map/ppermute | solution.py:485
  90.7 28.9 %collective-permute-done.9 = bf16[2,128,1024]{2,1,0:T(8,128)(2,1)S(1)} collective-permute-done((bf16[2,128,1024]{2,1,0:T(8,128)(2,1)S(1)}, bf16[2,128,1024]{2,1,0:T(8,128)(2,1)S(1)}, u32[]{:S(2)}, u32[]{:S(2)}) %collective-permute-start.9) | collective-permute-done | bytes 524320 | tf_op jit(solution)/shard_map/ppermute | solution.py:485
  131.4 5.6 %shard_map.195 = (bf16[512,512]{1,0:T(8,128)(2,1)S(1)}, f32[4,2,512]{2,1,0:T(2,128)S(1)}) custom-call(s32[1]{0:T(128)S(6)} %copy.59.limit_ref, bf16[512,1024]{1,0:T(8,128)(2,1)S(1)} %convolution_convert_fusion.q_ref.k_ref, bf16[512,1024]{1,0:T(8,128)(2,1)S(1)} %convolution_convert_fusion.q_ref.k_ref, bf16[512,512]{1,0:T(8,128)(2,1)S(1)} %convolution_convert_fusion.10.v_ref), custom_call_target="tpu_custom_call" | custom-call | flops 536870912 | bytes 2097152 | tf_op jit(solution)/shard_map/pallas_call | solution.py:148
  137.9 15.5 %collective-permute-done.11 = bf16[2,2,128,1024]{3,2,1,0:T(8,128)(2,1)} collective-permute-done((bf16[2,2,128,1024]{3,2,1,0:T(8,128)(2,1)}, bf16[2,2,128,1024]{3,2,1,0:T(8,128)(2,1)}, u32[]{:S(2)}, u32[]{:S(2)}) %collective-permute-start.11) | collective-permute-done | bytes 1048608 | tf_op jit(solution)/shard_map/ppermute | solution.py:485
  163.2 5.1 %collective-permute-done.12 = bf16[2,2,64,1024]{3,2,1,0:T(8,128)(2,1)} collective-permute-done((bf16[2,2,64,1024]{3,2,1,0:T(8,128)(2,1)}, bf16[2,2,64,1024]{3,2,1,0:T(8,128)(2,1)}, u32[]{:S(2)}, u32[]{:S(2)}) %collective-permute-start.12) | collective-permute-done | bytes 524320 | tf_op jit(solution)/shard_map/ppermute | solution.py:485
  175.2 2.8 shard_map.196
  180.6 3.4 copy-done.4
  185.6 3.5 shard_map.198
  190.7 2.7 collective-permute-done.15.other_ref
  194.5 5.3 %add_convert_fusion = (bf16[512,2048]{1,0:T(8,128)(2,1)}, bf16[512,2048]{1,0:T(8,128)(2,1)S(1)}) fusion(bf16[512,1024]{1,0:T(8,128)(2,1)S(1)} %get-tuple-element.164.x_ref, bf16[1024,2048]{1,0:T(8,128)(2,1)S(1)} %get-tuple-element.165), kind=kOutput, calls=%fused_computation.1 | convolution fusion | flops 2163212288 | bytes 9437184 | tf_op jit(solution)/shard_map/dot_general | solution.py:18
  210.7 5.2 %shard_map.201 = bf16[1024,2048]{1,0:T(8,128)(2,1)} custom-call(s32[16]{0:T(128)S(1)} %and_select_fusion.place_ref, bf16[512,1024]{1,0:T(8,128)(2,1)S(1)} %get-tuple-element.170.x_ref, bf16[512,2048]{1,0:T(8,128)(2,1)S(1)} %get-tuple-element.166.d_ref), custom_call_target="tpu_custom_call" | custom-call | flops 2147483648 | bytes 6291456 | tf_op jit(solution)/shard_map/pallas_call | solution.py:397
  216.9 5.6 %multiply_convert_fusion.d_ref = bf16[512,2048]{1,0:T(8,128)(2,1)S(1)} fusion(bf16[512,2048]{1,0:T(8,128)(2,1)} %get-tuple-element.171, bf16[512,1024]{1,0:T(8,128)(2,1)} %copy-done.29, bf16[1024,2048]{1,0:T(8,128)(2,1)} %copy-done.25), kind=kOutput, calls=%fused_computation | convolution fusion | flops 2150629376 | bytes 9437184 | tf_op jit(solution)/shard_map/dot_general | solution.py:18
  222.6 3.3 convolution_convert_fusion.4.own_ref
  228.9 5.2 %shard_map.210 = bf16[1024,2048]{1,0:T(8,128)(2,1)} custom-call(s32[16]{0:T(128)S(1)} %and_select_fusion.place_ref, bf16[512,1024]{1,0:T(8,128)(2,1)S(1)} %copy-done.27, bf16[512,2048]{1,0:T(8,128)(2,1)S(1)} %copy-done.31), custom_call_target="tpu_custom_call" | custom-call | flops 2147483648 | bytes 6291456 | tf_op jit(solution)/shard_map/pallas_call | solution.py:397
  234.2 3.1 fusion.27
  239.1 4.0 shard_map.202
  244.3 6.1 %shard_map.203 = (bf16[512,512]{1,0:T(8,128)(2,1)S(1)}, bf16[256,512]{1,0:T(8,128)(2,1)S(1)}, bf16[256,512]{1,0:T(8,128)(2,1)S(1)}) custom-call(s32[1]{0:T(128)S(6)} %copy.60.limit_ref, bf16[512,512]{1,0:T(8,128)(2,1)S(1)} %copy-done.35, bf16[256,1024]{1,0:T(8,128)(2,1)S(1)} %copy-done.33, bf16[256,1024]{1,0:T(8,128)(2,1)S(1)} %copy-done.33, ...), custom_call_target="tpu_custom_call" | custom-call | flops 671088640 | bytes 4194304 | tf_op jit(solution)/shard_map/pallas_call | solution.py:169
  254.0 3.7 shard_map.209
  266.0 8.2 %shard_map.205 = (bf16[512,512]{1,0:T(8,128)(2,1)S(1)}, bf16[512,512]{1,0:T(8,128)(2,1)S(1)}, bf16[512,512]{1,0:T(8,128)(2,1)S(1)}) custom-call(s32[1]{0:T(128)S(6)} %copy.59.limit_ref, bf16[512,1024]{1,0:T(8,128)(2,1)S(1)} %copy-done.39, bf16[512,1024]{1,0:T(8,128)(2,1)S(1)} %copy-done.39, bf16[512,512]{1,0:T(8,128)(2,1)S(1)} %copy-done.41, ...), custom_call_target="tpu_custom_call" | custom-call | flops 1342177280 | bytes 4194304 | tf_op jit(solution)/shard_map/pallas_call | solution.py:169
  290.4 11.6 %collective-permute-done.28 = bf16[2,4,128,512]{3,2,1,0:T(8,128)(2,1)S(1)} collective-permute-done((bf16[2,4,128,512]{3,2,1,0:T(8,128)(2,1)S(1)}, bf16[2,4,128,512]{3,2,1,0:T(8,128)(2,1)S(1)}, u32[]{:S(2)}, u32[]{:S(2)}) %collective-permute-start.28) | collective-permute-done | bytes 1048608 | tf_op jit(solution)/shard_map/ppermute | solution.py:485
  304.2 2.5 collective-permute-start.29
  315.2 2.8 collective-permute-done.42
  319.4 19.2 %collective-permute-done.37 = bf16[4,256,512]{2,1,0:T(8,128)(2,1)} collective-permute-done((bf16[4,256,512]{2,1,0:T(8,128)(2,1)}, bf16[4,256,512]{2,1,0:T(8,128)(2,1)}, u32[]{:S(2)}, u32[]{:S(2)}) %collective-permute-start.37) | collective-permute-done | bytes 1048608 | tf_op jit(solution)/shard_map/ppermute | solution.py:485
  340.5 2.7 add_convert_fusion.1
  347.6 8.3 %collective-permute-done.25 = bf16[2,256,512]{2,1,0:T(8,128)(2,1)} collective-permute-done((bf16[2,256,512]{2,1,0:T(8,128)(2,1)}, bf16[2,256,512]{2,1,0:T(8,128)(2,1)}, u32[]{:S(2)}, u32[]{:S(2)}) %collective-permute-start.25) | collective-permute-done | bytes 524320 | tf_op jit(solution)/shard_map/ppermute | solution.py:485
  378.3 24.0 %collective-permute-done.40 = bf16[2,64,2048]{2,1,0:T(8,128)(2,1)S(1)} collective-permute-done((bf16[2,64,2048]{2,1,0:T(8,128)(2,1)S(1)}, bf16[2,64,2048]{2,1,0:T(8,128)(2,1)S(1)}, u32[]{:S(2)}, u32[]{:S(2)}) %collective-permute-start.40) | collective-permute-done | bytes 524320 | tf_op jit(solution)/shard_map/ppermute | solution.py:485
  404.6 8.8 %collective-permute-done.41 = bf16[64,2048]{1,0:T(8,128)(2,1)S(1)} collective-permute-done((bf16[64,2048]{1,0:T(8,128)(2,1)S(1)}, bf16[64,2048]{1,0:T(8,128)(2,1)S(1)}, u32[]{:S(2)}, u32[]{:S(2)}) %collective-permute-start.41) | collective-permute-done | bytes 262176 | tf_op jit(solution)/shard_map/ppermute | solution.py:485
  (345 shorter events, 142.4 us)
Async XLA Ops:
  7.2 173.4 %all-gather.2.cloned.1.call-start = ((), (), s32[]{:S(2)}) async-start(), calls=%async_computation.3 | async-start | bytes 8912896 | tf_op jit(solution)/shard_map/all_gather | solution.py:631
  7.9 367.6 %reduce-scatter.8.cloned.1.call-start = ((), (), s32[]{:S(2)}) async-start(), calls=%async_computation.6 | async-start | bytes 5242880 | tf_op jit(solution)/shard_map/reduce_scatter | solution.py:562
  10.6 20.7 %collective-permute-start.1 = (bf16[136,1024]{1,0:T(8,128)(2,1)S(1)}, bf16[136,1024]{1,0:T(8,128)(2,1)S(1)}, u32[]{:S(2)}, u32[]{:S(2)}) collective-permute-start(bf16[136,1024]{1,0:T(8,128)(2,1)S(1)} %fusion.58), channel_id=1, source_target_pairs={{0,16},{2,18},{4,20},{6,22},{8,24},{10,26},{12,28},{14,30},{16,0},... | collective-permute-start | bytes 835592 | tf_op jit(solution)/shard_map/ppermute | solution.py:485
  15.7 42.2 %collective-permute-start = (bf16[256,1024]{1,0:T(8,128)(2,1)S(1)}, bf16[256,1024]{1,0:T(8,128)(2,1)}, u32[]{:S(2)}, u32[]{:S(2)}) collective-permute-start(bf16[256,1024]{1,0:T(8,128)(2,1)S(1)} %fusion.29), channel_id=1, source_target_pairs={{0,1},{1,0},{2,3},{3,2},{4,5},{5,4},{6,7},{7,6},{8,9},{9,8},{10,11... | collective-permute-start | bytes 1572872 | tf_op jit(solution)/shard_map/ppermute | solution.py:34
  31.4 24.5 %collective-permute-start.2 = (bf16[2,136,1024]{2,1,0:T(8,128)(2,1)S(1)}, bf16[2,136,1024]{2,1,0:T(8,128)(2,1)S(1)}, u32[]{:S(2)}, u32[]{:S(2)}) collective-permute-start(bf16[2,136,1024]{2,1,0:T(8,128)(2,1)S(1)} %get-tuple-element.147), channel_id=1, source_target_pairs={{0,8},{2,10},{4,12},{6,14},{8,0},{10,2},{12,4},{14,6},{16,24},{18,... | collective-permute-start | bytes 1671176 | tf_op jit(solution)/shard_map/ppermute | solution.py:485
  36.8 123.9 %collective-permute-start.13 = (bf16[128,1024]{1,0:T(8,128)(2,1)S(1)}, bf16[128,1024]{1,0:T(8,128)(2,1)}, u32[]{:S(2)}, u32[]{:S(2)}) collective-permute-start(bf16[128,1024]{1,0:T(8,128)(2,1)S(1)} %fusion.32), channel_id=1, source_target_pairs={{0,1},{1,0},{2,3},{3,2},{4,5},{5,4},{6,7},{7,6},{8,9},{9,8},{10,11... | collective-permute-start | bytes 786440 | tf_op jit(solution)/shard_map/ppermute | solution.py:34
  56.0 29.5 %collective-permute-start.3 = (bf16[2,2,136,1024]{3,2,1,0:T(8,128)(2,1)S(1)}, bf16[2,2,136,1024]{3,2,1,0:T(8,128)(2,1)S(1)}, u32[]{:S(2)}, u32[]{:S(2)}) collective-permute-start(bf16[2,2,136,1024]{3,2,1,0:T(8,128)(2,1)S(1)} %pad_maximum_fusion.4), channel_id=1, source_target_pairs={{0,4},{2,6},{4,0},{6,2},{8,12},{10,14},{12,8},{14,10},{16,20},{18,... | collective-permute-start | bytes 3342344 | tf_op jit(solution)/shard_map/ppermute | solution.py:485
  59.5 28.2 %collective-permute-start.4 = (bf16[2,2,136,1024]{3,2,1,0:T(8,128)(2,1)S(1)}, bf16[2,2,136,1024]{3,2,1,0:T(8,128)(2,1)S(1)}, u32[]{:S(2)}, u32[]{:S(2)}) collective-permute-start(bf16[2,2,136,1024]{3,2,1,0:T(8,128)(2,1)S(1)} %pad_maximum_fusion.4), channel_id=1, source_target_pairs={{0,2},{2,0},{4,6},{6,4},{8,10},{10,8},{12,14},{14,12},{16,18},{18,... | collective-permute-start | bytes 3342344 | tf_op jit(solution)/shard_map/ppermute | solution.py:485
  61.1 24.2 %collective-permute-start.8 = (bf16[128,1024]{1,0:T(8,128)(2,1)S(1)}, bf16[128,1024]{1,0:T(8,128)(2,1)S(1)}, u32[]{:S(2)}, u32[]{:S(2)}) collective-permute-start(bf16[128,1024]{1,0:T(8,128)(2,1)S(1)} %get-tuple-element.154), channel_id=1, source_target_pairs={{0,16},{2,18},{4,20},{6,22},{8,24},{10,26},{12,28},{14,30},{16,0},... | collective-permute-start | bytes 786440 | tf_op jit(solution)/shard_map/ppermute | solution.py:485
  85.3 34.3 %collective-permute-start.9 = (bf16[2,128,1024]{2,1,0:T(8,128)(2,1)S(1)}, bf16[2,128,1024]{2,1,0:T(8,128)(2,1)S(1)}, u32[]{:S(2)}, u32[]{:S(2)}) collective-permute-start(bf16[2,128,1024]{2,1,0:T(8,128)(2,1)S(1)} %get-tuple-element.155), channel_id=1, source_target_pairs={{0,8},{2,10},{4,12},{6,14},{8,0},{10,2},{12,4},{14,6},{16,24},{18,... | collective-permute-start | bytes 1572872 | tf_op jit(solution)/shard_map/ppermute | solution.py:485
  87.7 35.2 %collective-permute-start.6 = (bf16[2,2,64,1024]{3,2,1,0:T(8,128)(2,1)S(1)}, bf16[2,2,64,1024]{3,2,1,0:T(8,128)(2,1)S(1)}, u32[]{:S(2)}, u32[]{:S(2)}) collective-permute-start(bf16[2,2,64,1024]{3,2,1,0:T(8,128)(2,1)S(1)} %get-tuple-element.150), channel_id=1, source_target_pairs={{0,2},{2,0},{4,6},{6,4},{8,10},{10,8},{12,14},{14,12},{16,18},{18,... | collective-permute-start | bytes 1572872 | tf_op jit(solution)/shard_map/ppermute | solution.py:485
  88.9 35.5 %collective-permute-start.5 = (bf16[2,2,72,1024]{3,2,1,0:T(8,128)(2,1)S(1)}, bf16[2,2,72,1024]{3,2,1,0:T(8,128)(2,1)S(1)}, u32[]{:S(2)}, u32[]{:S(2)}) collective-permute-start(bf16[2,2,72,1024]{3,2,1,0:T(8,128)(2,1)S(1)} %slice.466), channel_id=1, source_target_pairs={{0,4},{2,6},{4,0},{6,2},{8,12},{10,14},{12,8},{14,10},{16,20},{18,... | collective-permute-start | bytes 1769480 | tf_op jit(solution)/shard_map/ppermute | solution.py:485
  120.8 32.7 %collective-permute-start.11 = (bf16[2,2,128,1024]{3,2,1,0:T(8,128)(2,1)}, bf16[2,2,128,1024]{3,2,1,0:T(8,128)(2,1)}, u32[]{:S(2)}, u32[]{:S(2)}) collective-permute-start(bf16[2,2,128,1024]{3,2,1,0:T(8,128)(2,1)} %pad_maximum_fusion.5), channel_id=1, source_target_pairs={{0,2},{2,0},{4,6},{6,4},{8,10},{10,8},{12,14},{14,12},{16,18},{18,... | collective-permute-start | bytes 3145736 | tf_op jit(solution)/shard_map/ppermute | solution.py:485
  121.2 34.6 %collective-permute-start.10 = (bf16[2,2,128,1024]{3,2,1,0:T(8,128)(2,1)}, bf16[2,2,128,1024]{3,2,1,0:T(8,128)(2,1)}, u32[]{:S(2)}, u32[]{:S(2)}) collective-permute-start(bf16[2,2,128,1024]{3,2,1,0:T(8,128)(2,1)} %pad_maximum_fusion.5), channel_id=1, source_target_pairs={{0,4},{2,6},{4,0},{6,2},{8,12},{10,14},{12,8},{14,10},{16,20},{18,... | collective-permute-start | bytes 3145736 | tf_op jit(solution)/shard_map/ppermute | solution.py:485
  137.8 36.9 %collective-permute-start.7 = (bf16[512,1024]{1,0:T(8,128)(2,1)S(1)}, bf16[512,1024]{1,0:T(8,128)(2,1)}, u32[]{:S(2)}, u32[]{:S(2)}) collective-permute-start(bf16[512,1024]{1,0:T(8,128)(2,1)S(1)} %convolution_convert_fusion.3.own_ref), channel_id=1, source_target_pairs={{0,1},{1,0},{2,3},{3,2},{4,5},{5,4},{6,7},{7,6},{8,9},{9,8},{10,11... | collective-permute-start | bytes 3145736 | tf_op jit(solution)/shard_map/ppermute | solution.py:34
  216.8 160.0 %reduce-scatter.4.cloned.1.call-start = ((), (), s32[]{:S(2)}) async-start(), calls=%async_computation.4 | async-start | bytes 5242880 | tf_op jit(solution)/shard_map/reduce_scatter | solution.py:562
  234.1 179.4 %reduce-scatter.6.cloned.1.call-start = ((), (), s32[]{:S(2)}) async-start(), calls=%async_computation.5 | async-start | bytes 1310720 | tf_op jit(solution)/shard_map/reduce_scatter | solution.py:567
  257.6 26.8 %collective-permute-start.34 = (bf16[2,256,512]{2,1,0:T(8,128)(2,1)S(1)}, bf16[2,256,512]{2,1,0:T(8,128)(2,1)S(1)}, u32[]{:S(2)}, u32[]{:S(2)}) collective-permute-start(bf16[2,256,512]{2,1,0:T(8,128)(2,1)S(1)} %get-tuple-element.199), channel_id=1, source_target_pairs={{0,2},{2,0},{4,6},{6,4},{8,10},{10,8},{12,14},{14,12},{16,18},{18,... | collective-permute-start | bytes 1572872 | tf_op jit(solution)/shard_map/ppermute | solution.py:485
  258.0 27.4 %collective-permute-start.35 = (bf16[2,256,512]{2,1,0:T(8,128)(2,1)S(1)}, bf16[2,256,512]{2,1,0:T(8,128)(2,1)S(1)}, u32[]{:S(2)}, u32[]{:S(2)}) collective-permute-start(bf16[2,256,512]{2,1,0:T(8,128)(2,1)S(1)} %get-tuple-element.200), channel_id=1, source_target_pairs={{0,4},{2,6},{4,0},{6,2},{8,12},{10,14},{12,8},{14,10},{16,20},{18,... | collective-permute-start | bytes 1572872 | tf_op jit(solution)/shard_map/ppermute | solution.py:485
  277.4 24.7 %collective-permute-start.28 = (bf16[2,4,128,512]{3,2,1,0:T(8,128)(2,1)S(1)}, bf16[2,4,128,512]{3,2,1,0:T(8,128)(2,1)S(1)}, u32[]{:S(2)}, u32[]{:S(2)}) collective-permute-start(bf16[2,4,128,512]{3,2,1,0:T(8,128)(2,1)S(1)} %get-tuple-element.194), channel_id=1, source_target_pairs={{0,8},{2,10},{4,12},{6,14},{8,0},{10,2},{12,4},{14,6},{16,24},{18,... | collective-permute-start | bytes 3145736 | tf_op jit(solution)/shard_map/ppermute | solution.py:485
  280.2 24.0 %collective-permute-start.20 = (bf16[512,1024]{1,0:T(8,128)(2,1)S(1)}, bf16[512,1024]{1,0:T(8,128)(2,1)S(1)}, u32[]{:S(2)}, u32[]{:S(2)}) collective-permute-start(bf16[512,1024]{1,0:T(8,128)(2,1)S(1)} %add_convert_fusion.3.own_ref), channel_id=1, source_target_pairs={{0,1},{1,0},{2,3},{3,2},{4,5},{5,4},{6,7},{7,6},{8,9},{9,8},{10,11... | collective-permute-start | bytes 3145736 | tf_op jit(solution)/shard_map/ppermute | solution.py:34
  284.1 24.8 %collective-permute-start.22 = (bf16[1,256,512]{2,1,0:T(8,128)(2,1)S(1)}, bf16[1,256,512]{2,1,0:T(8,128)(2,1)S(1)}, u32[]{:S(2)}, u32[]{:S(2)}) collective-permute-start(bf16[1,256,512]{2,1,0:T(8,128)(2,1)S(1)} %get-tuple-element.188), channel_id=1, source_target_pairs={{0,2},{2,0},{4,6},{6,4},{8,10},{10,8},{12,14},{14,12},{16,18},{18,... | collective-permute-start | bytes 786440 | tf_op jit(solution)/shard_map/ppermute | solution.py:485
  284.4 24.5 %collective-permute-start.23 = (bf16[1,256,512]{2,1,0:T(8,128)(2,1)S(1)}, bf16[1,256,512]{2,1,0:T(8,128)(2,1)S(1)}, u32[]{:S(2)}, u32[]{:S(2)}) collective-permute-start(bf16[1,256,512]{2,1,0:T(8,128)(2,1)S(1)} %get-tuple-element.189), channel_id=1, source_target_pairs={{0,4},{2,6},{4,0},{6,2},{8,12},{10,14},{12,8},{14,10},{16,20},{18,... | collective-permute-start | bytes 786440 | tf_op jit(solution)/shard_map/ppermute | solution.py:485
  287.4 51.2 %collective-permute-start.37 = (bf16[4,256,512]{2,1,0:T(8,128)(2,1)}, bf16[4,256,512]{2,1,0:T(8,128)(2,1)}, u32[]{:S(2)}, u32[]{:S(2)}) collective-permute-start(bf16[4,256,512]{2,1,0:T(8,128)(2,1)} %fusion.50), channel_id=1, source_target_pairs={{0,4},{2,6},{4,0},{6,2},{8,12},{10,14},{12,8},{14,10},{16,20},{18,... | collective-permute-start | bytes 3145736 | tf_op jit(solution)/shard_map/ppermute | solution.py:485
  302.0 38.5 %collective-permute-start.36 = (bf16[4,256,512]{2,1,0:T(8,128)(2,1)}, bf16[4,256,512]{2,1,0:T(8,128)(2,1)}, u32[]{:S(2)}, u32[]{:S(2)}) collective-permute-start(bf16[4,256,512]{2,1,0:T(8,128)(2,1)} %fusion.49), channel_id=1, source_target_pairs={{0,2},{2,0},{4,6},{6,4},{8,10},{10,8},{12,14},{14,12},{16,18},{18,... | collective-permute-start | bytes 3145736 | tf_op jit(solution)/shard_map/ppermute | solution.py:485
  304.2 40.0 %collective-permute-start.29 = (bf16[2,4,64,512]{3,2,1,0:T(8,128)(2,1)}, bf16[2,4,64,512]{3,2,1,0:T(8,128)(2,1)}, u32[]{:S(2)}, u32[]{:S(2)}) collective-permute-start(bf16[2,4,64,512]{3,2,1,0:T(8,128)(2,1)} %slice.498), channel_id=1, source_target_pairs={{0,16},{2,18},{4,20},{6,22},{8,24},{10,26},{12,28},{14,30},{16,0},... | collective-permute-start | bytes 1572872 | tf_op jit(solution)/shard_map/ppermute | solution.py:485
  310.6 45.3 %collective-permute-start.25 = (bf16[2,256,512]{2,1,0:T(8,128)(2,1)}, bf16[2,256,512]{2,1,0:T(8,128)(2,1)}, u32[]{:S(2)}, u32[]{:S(2)}) collective-permute-start(bf16[2,256,512]{2,1,0:T(8,128)(2,1)} %fusion.60), channel_id=1, source_target_pairs={{0,4},{2,6},{4,0},{6,2},{8,12},{10,14},{12,8},{14,10},{16,20},{18,... | collective-permute-start | bytes 1572872 | tf_op jit(solution)/shard_map/ppermute | solution.py:485
  318.0 37.9 %collective-permute-start.24 = (bf16[2,256,512]{2,1,0:T(8,128)(2,1)S(1)}, bf16[2,256,512]{2,1,0:T(8,128)(2,1)S(1)}, u32[]{:S(2)}, u32[]{:S(2)}) collective-permute-start(bf16[2,256,512]{2,1,0:T(8,128)(2,1)S(1)} %fusion.59), channel_id=1, source_target_pairs={{0,2},{2,0},{4,6},{6,4},{8,10},{10,8},{12,14},{14,12},{16,18},{18,... | collective-permute-start | bytes 1572872 | tf_op jit(solution)/shard_map/ppermute | solution.py:485
  343.3 18.1 %collective-permute-start.38 = (bf16[4,2,64,512]{3,2,1,0:T(8,128)(2,1)S(1)}, bf16[4,2,64,512]{3,2,1,0:T(8,128)(2,1)S(1)}, u32[]{:S(2)}, u32[]{:S(2)}) collective-permute-start(bf16[4,2,64,512]{3,2,1,0:T(8,128)(2,1)S(1)} %slice.509), channel_id=1, source_target_pairs={{0,8},{2,10},{4,12},{6,14},{8,0},{10,2},{12,4},{14,6},{16,24},{18,... | collective-permute-start | bytes 1572872 | tf_op jit(solution)/shard_map/ppermute | solution.py:485
  345.4 18.1 %collective-permute-start.30 = (bf16[1,64,512]{2,1,0:T(8,128)(2,1)S(1)}, bf16[1,64,512]{2,1,0:T(8,128)(2,1)S(1)}, u32[]{:S(2)}, u32[]{:S(2)}) collective-permute-start(bf16[1,64,512]{2,1,0:T(8,128)(2,1)S(1)} %get-tuple-element.239), channel_id=1, source_target_pairs={{0,2},{2,0},{4,6},{6,4},{8,10},{10,8},{12,14},{14,12},{16,18},{18,... | collective-permute-start | bytes 196616 | tf_op jit(solution)/shard_map/ppermute | solution.py:485
  371.6 31.2 %collective-permute-start.27 = (bf16[2,1,64,512]{3,2,0,1:T(8,128)(2,1)}, bf16[2,1,64,512]{3,2,0,1:T(8,128)(2,1)}, u32[]{:S(2)}, u32[]{:S(2)}) collective-permute-start(bf16[2,1,64,512]{3,2,0,1:T(8,128)(2,1)} %slice.496), channel_id=1, source_target_pairs={{0,16},{2,18},{4,20},{6,22},{8,24},{10,26},{12,28},{14,30},{16,0},... | collective-permute-start | bytes 393224 | tf_op jit(solution)/shard_map/ppermute | solution.py:485
  376.7 25.6 %collective-permute-start.40 = (bf16[2,64,2048]{2,1,0:T(8,128)(2,1)S(1)}, bf16[2,64,2048]{2,1,0:T(8,128)(2,1)S(1)}, u32[]{:S(2)}, u32[]{:S(2)}) collective-permute-start(bf16[2,64,2048]{2,1,0:T(8,128)(2,1)S(1)} %dynamic-slice_bitcast_fusion), channel_id=1, source_target_pairs={{0,8},{2,10},{4,12},{6,14},{8,0},{10,2},{12,4},{14,6},{16,24},{18,... | collective-permute-start | bytes 1572872 | tf_op jit(solution)/shard_map/ppermute | solution.py:485
  (84 other events, 537.4 us)
Sparse Core Ops, SparseCore 0:
  10.8 154.6 all-gather.1
  217.0 59.1 reduce-scatter.7
  279.4 83.7 reduce-scatter.3
  377.0 31.6 reduce-scatter.5

commit v2 on v1

--- a/solution.py
+++ b/solution.py
@@ -242,11 +242,11 @@
 
 def norm_rows(index, x, own, other, params):
     rows, width = x.shape
-    step = rows // 4
+    step = rows // 2
     row = row_spec(step, width)
     return pl.pallas_call(
         functools.partial(norm_kernel, index),
-        grid=(4,),
+        grid=(2,),
         in_specs=[row, row, row, fixed_spec(*params.shape)],
         out_specs=[row, row],
         out_shape=[
@@ -283,11 +283,11 @@
 
 def norm_last(limit, x, own, other, params, cot):
     rows, width = x.shape
-    step = rows // 4
+    step = rows // 2
     row = row_spec(step, width)
     return pl.pallas_call(
         last_kernel,
-        grid=(4,),
+        grid=(2,),
         in_specs=[SCALAR, row, row, row, fixed_spec(*params.shape), row],
         out_specs=[row, row, row, fixed_spec(2, width)],
         out_shape=[
@@ -321,12 +321,12 @@
 
 def norm_rows_back(index, x, own, other, dres, params):
     rows, width = x.shape
-    step = rows // 4
+    step = rows // 2
     row = row_spec(step, width)
     lower = 1 if index else 0
     return pl.pallas_call(
         functools.partial(back_kernel, index),
-        grid=(4,),
+        grid=(2,),
         in_specs=[row, row, row, row, fixed_spec(*params.shape)],
         out_specs=[row] + [row] * lower + [fixed_spec(2, width)],
         out_shape=[jax.ShapeDtypeStruct((rows, width), F32)]

time: 430 us -> 426 us (level)
  no operation moved by 1% of the time
where the time goes in v2:
time: 426 us; the launch traced here: 419 us
  waiting for transfers between devices  193 us (45%)
  Pallas kernels  55.1 us (13%)
  starting transfers between devices  49.4 us (12%)
  matrix products  39.9 us (9%)
  local copies, waits for them, and re-layouts  34.4 us (8%)
  other arithmetic  30.4 us (7%)
  between operations  16.9 us (4%)
    ppermute x36, waiting for transfers between devices, hop(): return lax.ppermute(values, 'dp', [(i, i ^ 1 << bit) for i in range(n_dp)])  188 us
    ppermute x36, starting transfers between devices, hop(): return lax.ppermute(values, 'dp', [(i, i ^ 1 << bit) for i in range(n_dp)])  47.6 us
    dot_general x25, matrix products, dot(): return lax.dot_general(a, b, (dims, ((), ())), preferred_element_type=F32)  39.9 us
    unnamed x134, local copies, waits for them, and re-layouts  20.9 us
    pallas_call x2, Pallas kernels, attend_back(): pl.pallas_call(functools.partial(backward_kernel, causal), grid=(pairs,),...  14.5 us
    pallas_call x2, Pallas kernels, outer(): pl.pallas_call(outer_kernel, grid=(FFN_STEPS,), in_specs=[SCALAR, fixed_s...  10.4 us
    pallas_call x2, Pallas kernels, attend(): pl.pallas_call(functools.partial(forward_kernel, causal), grid=(pairs,),...  9.11 us
  transfers between devices with their start and end apart: 50, of which 22 were waited for; matrix products, arithmetic and copies ran while one was open for 17% of the time, Pallas kernels for 10%

profile of v2, /device:TPU:0, one launch (start us, length us, event | category | flops | bytes accessed | tf_op | source)
XLA Modules:
  0.0 419.2 jit_solution(3089683941805064359)
XLA Ops:
  10.6 4.1 collective-permute-start.1
  15.8 15.5 %collective-permute-done.1 = bf16[136,1024]{1,0:T(8,128)(2,1)S(1)} collective-permute-done((bf16[136,1024]{1,0:T(8,128)(2,1)S(1)}, bf16[136,1024]{1,0:T(8,128)(2,1)S(1)}, u32[]{:S(2)}, u32[]{:S(2)}) %collective-permute-start.1) | collective-permute-done | bytes 278560 | tf_op jit(solution)/shard_map/ppermute | solution.py:485
  31.4 4.6 %collective-permute-start.2 = (bf16[2,136,1024]{2,1,0:T(8,128)(2,1)S(1)}, bf16[2,136,1024]{2,1,0:T(8,128)(2,1)S(1)}, u32[]{:S(2)}, u32[]{:S(2)}) collective-permute-start(bf16[2,136,1024]{2,1,0:T(8,128)(2,1)S(1)} %get-tuple-element.147), channel_id=1, source_target_pairs={{0,8},{2,10},{4,12},{6,14},{8,0},{10,2},{12,4},{14,6},{16,24},{18,... | collective-permute-start | bytes 1671176 | tf_op jit(solution)/shard_map/ppermute | solution.py:485
  37.7 18.2 %collective-permute-done.2 = bf16[2,136,1024]{2,1,0:T(8,128)(2,1)S(1)} collective-permute-done((bf16[2,136,1024]{2,1,0:T(8,128)(2,1)S(1)}, bf16[2,136,1024]{2,1,0:T(8,128)(2,1)S(1)}, u32[]{:S(2)}, u32[]{:S(2)}) %collective-permute-start.2) | collective-permute-done | bytes 557088 | tf_op jit(solution)/shard_map/ppermute | solution.py:485
  61.1 3.7 collective-permute-start.8
  65.2 20.0 %collective-permute-done.8 = bf16[128,1024]{1,0:T(8,128)(2,1)S(1)} collective-permute-done((bf16[128,1024]{1,0:T(8,128)(2,1)S(1)}, bf16[128,1024]{1,0:T(8,128)(2,1)S(1)}, u32[]{:S(2)}, u32[]{:S(2)}) %collective-permute-start.8) | collective-permute-done | bytes 262176 | tf_op jit(solution)/shard_map/ppermute | solution.py:485
  90.7 28.9 %collective-permute-done.9 = bf16[2,128,1024]{2,1,0:T(8,128)(2,1)S(1)} collective-permute-done((bf16[2,128,1024]{2,1,0:T(8,128)(2,1)S(1)}, bf16[2,128,1024]{2,1,0:T(8,128)(2,1)S(1)}, u32[]{:S(2)}, u32[]{:S(2)}) %collective-permute-start.9) | collective-permute-done | bytes 524320 | tf_op jit(solution)/shard_map/ppermute | solution.py:485
  131.4 5.6 %shard_map.195 = (bf16[512,512]{1,0:T(8,128)(2,1)S(1)}, f32[4,2,512]{2,1,0:T(2,128)S(1)}) custom-call(s32[1]{0:T(128)S(6)} %copy.59.limit_ref, bf16[512,1024]{1,0:T(8,128)(2,1)S(1)} %convolution_convert_fusion.q_ref.k_ref, bf16[512,1024]{1,0:T(8,128)(2,1)S(1)} %convolution_convert_fusion.q_ref.k_ref, bf16[512,512]{1,0:T(8,128)(2,1)S(1)} %convolution_convert_fusion.10.v_ref), custom_call_target="tpu_custom_call" | custom-call | flops 536870912 | bytes 2097152 | tf_op jit(solution)/shard_map/pallas_call | solution.py:148
  137.9 15.5 %collective-permute-done.11 = bf16[2,2,128,1024]{3,2,1,0:T(8,128)(2,1)} collective-permute-done((bf16[2,2,128,1024]{3,2,1,0:T(8,128)(2,1)}, bf16[2,2,128,1024]{3,2,1,0:T(8,128)(2,1)}, u32[]{:S(2)}, u32[]{:S(2)}) %collective-permute-start.11) | collective-permute-done | bytes 1048608 | tf_op jit(solution)/shard_map/ppermute | solution.py:485
  163.2 5.1 %collective-permute-done.12 = bf16[2,2,64,1024]{3,2,1,0:T(8,128)(2,1)} collective-permute-done((bf16[2,2,64,1024]{3,2,1,0:T(8,128)(2,1)}, bf16[2,2,64,1024]{3,2,1,0:T(8,128)(2,1)}, u32[]{:S(2)}, u32[]{:S(2)}) %collective-permute-start.12) | collective-permute-done | bytes 524320 | tf_op jit(solution)/shard_map/ppermute | solution.py:485
  179.8 3.4 copy-done.4
  184.8 3.5 shard_map.198
  189.9 2.7 collective-permute-done.15.other_ref
  193.5 5.3 %add_convert_fusion = (bf16[512,2048]{1,0:T(8,128)(2,1)}, bf16[512,2048]{1,0:T(8,128)(2,1)S(1)}) fusion(bf16[512,1024]{1,0:T(8,128)(2,1)S(1)} %get-tuple-element.164.x_ref, bf16[1024,2048]{1,0:T(8,128)(2,1)S(1)} %get-tuple-element.165), kind=kOutput, calls=%fused_computation.1 | convolution fusion | flops 2163212288 | bytes 9437184 | tf_op jit(solution)/shard_map/dot_general | solution.py:18
  198.9 2.4 convolution_convert_fusion.5.own_ref
  209.7 5.2 %shard_map.201 = bf16[1024,2048]{1,0:T(8,128)(2,1)} custom-call(s32[16]{0:T(128)S(1)} %and_select_fusion.place_ref, bf16[512,1024]{1,0:T(8,128)(2,1)S(1)} %get-tuple-element.170.x_ref, bf16[512,2048]{1,0:T(8,128)(2,1)S(1)} %get-tuple-element.166.d_ref), custom_call_target="tpu_custom_call" | custom-call | flops 2147483648 | bytes 6291456 | tf_op jit(solution)/shard_map/pallas_call | solution.py:397
  215.9 5.6 %multiply_convert_fusion.d_ref = bf16[512,2048]{1,0:T(8,128)(2,1)S(1)} fusion(bf16[512,2048]{1,0:T(8,128)(2,1)} %get-tuple-element.171, bf16[512,1024]{1,0:T(8,128)(2,1)} %copy-done.29, bf16[1024,2048]{1,0:T(8,128)(2,1)} %copy-done.25), kind=kOutput, calls=%fused_computation | convolution fusion | flops 2150629376 | bytes 9437184 | tf_op jit(solution)/shard_map/dot_general | solution.py:18
  221.6 3.3 convolution_convert_fusion.4.own_ref
  227.9 5.2 %shard_map.210 = bf16[1024,2048]{1,0:T(8,128)(2,1)} custom-call(s32[16]{0:T(128)S(1)} %and_select_fusion.place_ref, bf16[512,1024]{1,0:T(8,128)(2,1)S(1)} %copy-done.27, bf16[512,2048]{1,0:T(8,128)(2,1)S(1)} %copy-done.31), custom_call_target="tpu_custom_call" | custom-call | flops 2147483648 | bytes 6291456 | tf_op jit(solution)/shard_map/pallas_call | solution.py:397
  233.2 3.1 fusion.27
  238.1 3.3 shard_map.202
  242.6 6.1 %shard_map.203 = (bf16[512,512]{1,0:T(8,128)(2,1)S(1)}, bf16[256,512]{1,0:T(8,128)(2,1)S(1)}, bf16[256,512]{1,0:T(8,128)(2,1)S(1)}) custom-call(s32[1]{0:T(128)S(6)} %copy.60.limit_ref, bf16[512,512]{1,0:T(8,128)(2,1)S(1)} %copy-done.35, bf16[256,1024]{1,0:T(8,128)(2,1)S(1)} %copy-done.33, bf16[256,1024]{1,0:T(8,128)(2,1)S(1)} %copy-done.33, ...), custom_call_target="tpu_custom_call" | custom-call | flops 671088640 | bytes 4194304 | tf_op jit(solution)/shard_map/pallas_call | solution.py:169
  252.3 3.7 shard_map.209
  264.0 8.4 %shard_map.205 = (bf16[512,512]{1,0:T(8,128)(2,1)S(1)}, bf16[512,512]{1,0:T(8,128)(2,1)S(1)}, bf16[512,512]{1,0:T(8,128)(2,1)S(1)}) custom-call(s32[1]{0:T(128)S(6)} %copy.59.limit_ref, bf16[512,1024]{1,0:T(8,128)(2,1)S(1)} %copy-done.39, bf16[512,1024]{1,0:T(8,128)(2,1)S(1)} %copy-done.39, bf16[512,512]{1,0:T(8,128)(2,1)S(1)} %copy-done.41, ...), custom_call_target="tpu_custom_call" | custom-call | flops 1342177280 | bytes 4194304 | tf_op jit(solution)/shard_map/pallas_call | solution.py:169
  288.6 11.5 %collective-permute-done.28 = bf16[2,4,128,512]{3,2,1,0:T(8,128)(2,1)S(1)} collective-permute-done((bf16[2,4,128,512]{3,2,1,0:T(8,128)(2,1)S(1)}, bf16[2,4,128,512]{3,2,1,0:T(8,128)(2,1)S(1)}, u32[]{:S(2)}, u32[]{:S(2)}) %collective-permute-start.28) | collective-permute-done | bytes 1048608 | tf_op jit(solution)/shard_map/ppermute | solution.py:485
  302.2 2.6 collective-permute-start.29
  313.1 3.1 collective-permute-done.42
  317.4 19.2 %collective-permute-done.37 = bf16[4,256,512]{2,1,0:T(8,128)(2,1)} collective-permute-done((bf16[4,256,512]{2,1,0:T(8,128)(2,1)}, bf16[4,256,512]{2,1,0:T(8,128)(2,1)}, u32[]{:S(2)}, u32[]{:S(2)}) %collective-permute-start.37) | collective-permute-done | bytes 1048608 | tf_op jit(solution)/shard_map/ppermute | solution.py:485
  345.7 6.7 %collective-permute-done.25 = bf16[2,256,512]{2,1,0:T(8,128)(2,1)} collective-permute-done((bf16[2,256,512]{2,1,0:T(8,128)(2,1)}, bf16[2,256,512]{2,1,0:T(8,128)(2,1)}, u32[]{:S(2)}, u32[]{:S(2)}) %collective-permute-start.25) | collective-permute-done | bytes 524320 | tf_op jit(solution)/shard_map/ppermute | solution.py:485
  369.4 2.5 collective-permute-done.39
  374.8 25.6 %collective-permute-done.40 = bf16[2,64,2048]{2,1,0:T(8,128)(2,1)S(1)} collective-permute-done((bf16[2,64,2048]{2,1,0:T(8,128)(2,1)S(1)}, bf16[2,64,2048]{2,1,0:T(8,128)(2,1)S(1)}, u32[]{:S(2)}, u32[]{:S(2)}) %collective-permute-start.40) | collective-permute-done | bytes 524320 | tf_op jit(solution)/shard_map/ppermute | solution.py:485
  402.4 7.7 %collective-permute-done.41 = bf16[64,2048]{1,0:T(8,128)(2,1)S(1)} collective-permute-done((bf16[64,2048]{1,0:T(8,128)(2,1)S(1)}, bf16[64,2048]{1,0:T(8,128)(2,1)S(1)}, u32[]{:S(2)}, u32[]{:S(2)}) %collective-permute-start.41) | collective-permute-done | bytes 262176 | tf_op jit(solution)/shard_map/ppermute | solution.py:485
  (345 shorter events, 140.8 us)
Async XLA Ops:
  7.2 172.6 %all-gather.2.cloned.1.call-start = ((), (), s32[]{:S(2)}) async-start(), calls=%async_computation.3 | async-start | bytes 8912896 | tf_op jit(solution)/shard_map/all_gather | solution.py:631
  7.9 364.1 %reduce-scatter.8.cloned.1.call-start = ((), (), s32[]{:S(2)}) async-start(), calls=%async_computation.6 | async-start | bytes 5242880 | tf_op jit(solution)/shard_map/reduce_scatter | solution.py:562
  10.6 20.7 %collective-permute-start.1 = (bf16[136,1024]{1,0:T(8,128)(2,1)S(1)}, bf16[136,1024]{1,0:T(8,128)(2,1)S(1)}, u32[]{:S(2)}, u32[]{:S(2)}) collective-permute-start(bf16[136,1024]{1,0:T(8,128)(2,1)S(1)} %fusion.58), channel_id=1, source_target_pairs={{0,16},{2,18},{4,20},{6,22},{8,24},{10,26},{12,28},{14,30},{16,0},... | collective-permute-start | bytes 835592 | tf_op jit(solution)/shard_map/ppermute | solution.py:485
  15.7 42.2 %collective-permute-start = (bf16[256,1024]{1,0:T(8,128)(2,1)S(1)}, bf16[256,1024]{1,0:T(8,128)(2,1)}, u32[]{:S(2)}, u32[]{:S(2)}) collective-permute-start(bf16[256,1024]{1,0:T(8,128)(2,1)S(1)} %fusion.29), channel_id=1, source_target_pairs={{0,1},{1,0},{2,3},{3,2},{4,5},{5,4},{6,7},{7,6},{8,9},{9,8},{10,11... | collective-permute-start | bytes 1572872 | tf_op jit(solution)/shard_map/ppermute | solution.py:34
  31.4 24.5 %collective-permute-start.2 = (bf16[2,136,1024]{2,1,0:T(8,128)(2,1)S(1)}, bf16[2,136,1024]{2,1,0:T(8,128)(2,1)S(1)}, u32[]{:S(2)}, u32[]{:S(2)}) collective-permute-start(bf16[2,136,1024]{2,1,0:T(8,128)(2,1)S(1)} %get-tuple-element.147), channel_id=1, source_target_pairs={{0,8},{2,10},{4,12},{6,14},{8,0},{10,2},{12,4},{14,6},{16,24},{18,... | collective-permute-start | bytes 1671176 | tf_op jit(solution)/shard_map/ppermute | solution.py:485
  36.8 123.9 %collective-permute-start.13 = (bf16[128,1024]{1,0:T(8,128)(2,1)S(1)}, bf16[128,1024]{1,0:T(8,128)(2,1)}, u32[]{:S(2)}, u32[]{:S(2)}) collective-permute-start(bf16[128,1024]{1,0:T(8,128)(2,1)S(1)} %fusion.32), channel_id=1, source_target_pairs={{0,1},{1,0},{2,3},{3,2},{4,5},{5,4},{6,7},{7,6},{8,9},{9,8},{10,11... | collective-permute-start | bytes 786440 | tf_op jit(solution)/shard_map/ppermute | solution.py:34
  56.0 29.5 %collective-permute-start.3 = (bf16[2,2,136,1024]{3,2,1,0:T(8,128)(2,1)S(1)}, bf16[2,2,136,1024]{3,2,1,0:T(8,128)(2,1)S(1)}, u32[]{:S(2)}, u32[]{:S(2)}) collective-permute-start(bf16[2,2,136,1024]{3,2,1,0:T(8,128)(2,1)S(1)} %pad_maximum_fusion.4), channel_id=1, source_target_pairs={{0,4},{2,6},{4,0},{6,2},{8,12},{10,14},{12,8},{14,10},{16,20},{18,... | collective-permute-start | bytes 3342344 | tf_op jit(solution)/shard_map/ppermute | solution.py:485
  59.5 28.2 %collective-permute-start.4 = (bf16[2,2,136,1024]{3,2,1,0:T(8,128)(2,1)S(1)}, bf16[2,2,136,1024]{3,2,1,0:T(8,128)(2,1)S(1)}, u32[]{:S(2)}, u32[]{:S(2)}) collective-permute-start(bf16[2,2,136,1024]{3,2,1,0:T(8,128)(2,1)S(1)} %pad_maximum_fusion.4), channel_id=1, source_target_pairs={{0,2},{2,0},{4,6},{6,4},{8,10},{10,8},{12,14},{14,12},{16,18},{18,... | collective-permute-start | bytes 3342344 | tf_op jit(solution)/shard_map/ppermute | solution.py:485
  61.1 24.2 %collective-permute-start.8 = (bf16[128,1024]{1,0:T(8,128)(2,1)S(1)}, bf16[128,1024]{1,0:T(8,128)(2,1)S(1)}, u32[]{:S(2)}, u32[]{:S(2)}) collective-permute-start(bf16[128,1024]{1,0:T(8,128)(2,1)S(1)} %get-tuple-element.154), channel_id=1, source_target_pairs={{0,16},{2,18},{4,20},{6,22},{8,24},{10,26},{12,28},{14,30},{16,0},... | collective-permute-start | bytes 786440 | tf_op jit(solution)/shard_map/ppermute | solution.py:485
  85.3 34.3 %collective-permute-start.9 = (bf16[2,128,1024]{2,1,0:T(8,128)(2,1)S(1)}, bf16[2,128,1024]{2,1,0:T(8,128)(2,1)S(1)}, u32[]{:S(2)}, u32[]{:S(2)}) collective-permute-start(bf16[2,128,1024]{2,1,0:T(8,128)(2,1)S(1)} %get-tuple-element.155), channel_id=1, source_target_pairs={{0,8},{2,10},{4,12},{6,14},{8,0},{10,2},{12,4},{14,6},{16,24},{18,... | collective-permute-start | bytes 1572872 | tf_op jit(solution)/shard_map/ppermute | solution.py:485
  87.7 35.2 %collective-permute-start.6 = (bf16[2,2,64,1024]{3,2,1,0:T(8,128)(2,1)S(1)}, bf16[2,2,64,1024]{3,2,1,0:T(8,128)(2,1)S(1)}, u32[]{:S(2)}, u32[]{:S(2)}) collective-permute-start(bf16[2,2,64,1024]{3,2,1,0:T(8,128)(2,1)S(1)} %get-tuple-element.150), channel_id=1, source_target_pairs={{0,2},{2,0},{4,6},{6,4},{8,10},{10,8},{12,14},{14,12},{16,18},{18,... | collective-permute-start | bytes 1572872 | tf_op jit(solution)/shard_map/ppermute | solution.py:485
  88.9 35.5 %collective-permute-start.5 = (bf16[2,2,72,1024]{3,2,1,0:T(8,128)(2,1)S(1)}, bf16[2,2,72,1024]{3,2,1,0:T(8,128)(2,1)S(1)}, u32[]{:S(2)}, u32[]{:S(2)}) collective-permute-start(bf16[2,2,72,1024]{3,2,1,0:T(8,128)(2,1)S(1)} %slice.466), channel_id=1, source_target_pairs={{0,4},{2,6},{4,0},{6,2},{8,12},{10,14},{12,8},{14,10},{16,20},{18,... | collective-permute-start | bytes 1769480 | tf_op jit(solution)/shard_map/ppermute | solution.py:485
  120.8 32.7 %collective-permute-start.11 = (bf16[2,2,128,1024]{3,2,1,0:T(8,128)(2,1)}, bf16[2,2,128,1024]{3,2,1,0:T(8,128)(2,1)}, u32[]{:S(2)}, u32[]{:S(2)}) collective-permute-start(bf16[2,2,128,1024]{3,2,1,0:T(8,128)(2,1)} %pad_maximum_fusion.5), channel_id=1, source_target_pairs={{0,2},{2,0},{4,6},{6,4},{8,10},{10,8},{12,14},{14,12},{16,18},{18,... | collective-permute-start | bytes 3145736 | tf_op jit(solution)/shard_map/ppermute | solution.py:485
  121.2 34.6 %collective-permute-start.10 = (bf16[2,2,128,1024]{3,2,1,0:T(8,128)(2,1)}, bf16[2,2,128,1024]{3,2,1,0:T(8,128)(2,1)}, u32[]{:S(2)}, u32[]{:S(2)}) collective-permute-start(bf16[2,2,128,1024]{3,2,1,0:T(8,128)(2,1)} %pad_maximum_fusion.5), channel_id=1, source_target_pairs={{0,4},{2,6},{4,0},{6,2},{8,12},{10,14},{12,8},{14,10},{16,20},{18,... | collective-permute-start | bytes 3145736 | tf_op jit(solution)/shard_map/ppermute | solution.py:485
  137.8 36.9 %collective-permute-start.7 = (bf16[512,1024]{1,0:T(8,128)(2,1)S(1)}, bf16[512,1024]{1,0:T(8,128)(2,1)}, u32[]{:S(2)}, u32[]{:S(2)}) collective-permute-start(bf16[512,1024]{1,0:T(8,128)(2,1)S(1)} %convolution_convert_fusion.3.own_ref), channel_id=1, source_target_pairs={{0,1},{1,0},{2,3},{3,2},{4,5},{5,4},{6,7},{7,6},{8,9},{9,8},{10,11... | collective-permute-start | bytes 3145736 | tf_op jit(solution)/shard_map/ppermute | solution.py:34
  215.8 157.5 %reduce-scatter.4.cloned.1.call-start = ((), (), s32[]{:S(2)}) async-start(), calls=%async_computation.4 | async-start | bytes 5242880 | tf_op jit(solution)/shard_map/reduce_scatter | solution.py:562
  233.1 177.1 %reduce-scatter.6.cloned.1.call-start = ((), (), s32[]{:S(2)}) async-start(), calls=%async_computation.5 | async-start | bytes 1310720 | tf_op jit(solution)/shard_map/reduce_scatter | solution.py:567
  255.9 26.5 %collective-permute-start.34 = (bf16[2,256,512]{2,1,0:T(8,128)(2,1)S(1)}, bf16[2,256,512]{2,1,0:T(8,128)(2,1)S(1)}, u32[]{:S(2)}, u32[]{:S(2)}) collective-permute-start(bf16[2,256,512]{2,1,0:T(8,128)(2,1)S(1)} %get-tuple-element.199), channel_id=1, source_target_pairs={{0,2},{2,0},{4,6},{6,4},{8,10},{10,8},{12,14},{14,12},{16,18},{18,... | collective-permute-start | bytes 1572872 | tf_op jit(solution)/shard_map/ppermute | solution.py:485
  256.3 27.1 %collective-permute-start.35 = (bf16[2,256,512]{2,1,0:T(8,128)(2,1)S(1)}, bf16[2,256,512]{2,1,0:T(8,128)(2,1)S(1)}, u32[]{:S(2)}, u32[]{:S(2)}) collective-permute-start(bf16[2,256,512]{2,1,0:T(8,128)(2,1)S(1)} %get-tuple-element.200), channel_id=1, source_target_pairs={{0,4},{2,6},{4,0},{6,2},{8,12},{10,14},{12,8},{14,10},{16,20},{18,... | collective-permute-start | bytes 1572872 | tf_op jit(solution)/shard_map/ppermute | solution.py:485
  275.3 24.8 %collective-permute-start.28 = (bf16[2,4,128,512]{3,2,1,0:T(8,128)(2,1)S(1)}, bf16[2,4,128,512]{3,2,1,0:T(8,128)(2,1)S(1)}, u32[]{:S(2)}, u32[]{:S(2)}) collective-permute-start(bf16[2,4,128,512]{3,2,1,0:T(8,128)(2,1)S(1)} %get-tuple-element.194), channel_id=1, source_target_pairs={{0,8},{2,10},{4,12},{6,14},{8,0},{10,2},{12,4},{14,6},{16,24},{18,... | collective-permute-start | bytes 3145736 | tf_op jit(solution)/shard_map/ppermute | solution.py:485
  278.2 24.1 %collective-permute-start.20 = (bf16[512,1024]{1,0:T(8,128)(2,1)S(1)}, bf16[512,1024]{1,0:T(8,128)(2,1)S(1)}, u32[]{:S(2)}, u32[]{:S(2)}) collective-permute-start(bf16[512,1024]{1,0:T(8,128)(2,1)S(1)} %add_convert_fusion.3.own_ref), channel_id=1, source_target_pairs={{0,1},{1,0},{2,3},{3,2},{4,5},{5,4},{6,7},{7,6},{8,9},{9,8},{10,11... | collective-permute-start | bytes 3145736 | tf_op jit(solution)/shard_map/ppermute | solution.py:34
  282.1 24.7 %collective-permute-start.22 = (bf16[1,256,512]{2,1,0:T(8,128)(2,1)S(1)}, bf16[1,256,512]{2,1,0:T(8,128)(2,1)S(1)}, u32[]{:S(2)}, u32[]{:S(2)}) collective-permute-start(bf16[1,256,512]{2,1,0:T(8,128)(2,1)S(1)} %get-tuple-element.188), channel_id=1, source_target_pairs={{0,2},{2,0},{4,6},{6,4},{8,10},{10,8},{12,14},{14,12},{16,18},{18,... | collective-permute-start | bytes 786440 | tf_op jit(solution)/shard_map/ppermute | solution.py:485
  282.5 24.3 %collective-permute-start.23 = (bf16[1,256,512]{2,1,0:T(8,128)(2,1)S(1)}, bf16[1,256,512]{2,1,0:T(8,128)(2,1)S(1)}, u32[]{:S(2)}, u32[]{:S(2)}) collective-permute-start(bf16[1,256,512]{2,1,0:T(8,128)(2,1)S(1)} %get-tuple-element.189), channel_id=1, source_target_pairs={{0,4},{2,6},{4,0},{6,2},{8,12},{10,14},{12,8},{14,10},{16,20},{18,... | collective-permute-start | bytes 786440 | tf_op jit(solution)/shard_map/ppermute | solution.py:485
  285.4 51.2 %collective-permute-start.37 = (bf16[4,256,512]{2,1,0:T(8,128)(2,1)}, bf16[4,256,512]{2,1,0:T(8,128)(2,1)}, u32[]{:S(2)}, u32[]{:S(2)}) collective-permute-start(bf16[4,256,512]{2,1,0:T(8,128)(2,1)} %fusion.50), channel_id=1, source_target_pairs={{0,4},{2,6},{4,0},{6,2},{8,12},{10,14},{12,8},{14,10},{16,20},{18,... | collective-permute-start | bytes 3145736 | tf_op jit(solution)/shard_map/ppermute | solution.py:485
  300.2 38.6 %collective-permute-start.36 = (bf16[4,256,512]{2,1,0:T(8,128)(2,1)}, bf16[4,256,512]{2,1,0:T(8,128)(2,1)}, u32[]{:S(2)}, u32[]{:S(2)}) collective-permute-start(bf16[4,256,512]{2,1,0:T(8,128)(2,1)} %fusion.49), channel_id=1, source_target_pairs={{0,2},{2,0},{4,6},{6,4},{8,10},{10,8},{12,14},{14,12},{16,18},{18,... | collective-permute-start | bytes 3145736 | tf_op jit(solution)/shard_map/ppermute | solution.py:485
  302.2 39.8 %collective-permute-start.29 = (bf16[2,4,64,512]{3,2,1,0:T(8,128)(2,1)}, bf16[2,4,64,512]{3,2,1,0:T(8,128)(2,1)}, u32[]{:S(2)}, u32[]{:S(2)}) collective-permute-start(bf16[2,4,64,512]{3,2,1,0:T(8,128)(2,1)} %slice.498), channel_id=1, source_target_pairs={{0,16},{2,18},{4,20},{6,22},{8,24},{10,26},{12,28},{14,30},{16,0},... | collective-permute-start | bytes 1572872 | tf_op jit(solution)/shard_map/ppermute | solution.py:485
  308.5 43.9 %collective-permute-start.25 = (bf16[2,256,512]{2,1,0:T(8,128)(2,1)}, bf16[2,256,512]{2,1,0:T(8,128)(2,1)}, u32[]{:S(2)}, u32[]{:S(2)}) collective-permute-start(bf16[2,256,512]{2,1,0:T(8,128)(2,1)} %fusion.60), channel_id=1, source_target_pairs={{0,4},{2,6},{4,0},{6,2},{8,12},{10,14},{12,8},{14,10},{16,20},{18,... | collective-permute-start | bytes 1572872 | tf_op jit(solution)/shard_map/ppermute | solution.py:485
  316.2 36.2 %collective-permute-start.24 = (bf16[2,256,512]{2,1,0:T(8,128)(2,1)S(1)}, bf16[2,256,512]{2,1,0:T(8,128)(2,1)S(1)}, u32[]{:S(2)}, u32[]{:S(2)}) collective-permute-start(bf16[2,256,512]{2,1,0:T(8,128)(2,1)S(1)} %fusion.59), channel_id=1, source_target_pairs={{0,2},{2,0},{4,6},{6,4},{8,10},{10,8},{12,14},{14,12},{16,18},{18,... | collective-permute-start | bytes 1572872 | tf_op jit(solution)/shard_map/ppermute | solution.py:485
  340.9 17.0 %collective-permute-start.38 = (bf16[4,2,64,512]{3,2,1,0:T(8,128)(2,1)S(1)}, bf16[4,2,64,512]{3,2,1,0:T(8,128)(2,1)S(1)}, u32[]{:S(2)}, u32[]{:S(2)}) collective-permute-start(bf16[4,2,64,512]{3,2,1,0:T(8,128)(2,1)S(1)} %slice.509), channel_id=1, source_target_pairs={{0,8},{2,10},{4,12},{6,14},{8,0},{10,2},{12,4},{14,6},{16,24},{18,... | collective-permute-start | bytes 1572872 | tf_op jit(solution)/shard_map/ppermute | solution.py:485
  343.3 16.8 %collective-permute-start.30 = (bf16[1,64,512]{2,1,0:T(8,128)(2,1)S(1)}, bf16[1,64,512]{2,1,0:T(8,128)(2,1)S(1)}, u32[]{:S(2)}, u32[]{:S(2)}) collective-permute-start(bf16[1,64,512]{2,1,0:T(8,128)(2,1)S(1)} %get-tuple-element.239), channel_id=1, source_target_pairs={{0,2},{2,0},{4,6},{6,4},{8,10},{10,8},{12,14},{14,12},{16,18},{18,... | collective-permute-start | bytes 196616 | tf_op jit(solution)/shard_map/ppermute | solution.py:485
  368.2 32.4 %collective-permute-start.27 = (bf16[2,1,64,512]{3,2,0,1:T(8,128)(2,1)}, bf16[2,1,64,512]{3,2,0,1:T(8,128)(2,1)}, u32[]{:S(2)}, u32[]{:S(2)}) collective-permute-start(bf16[2,1,64,512]{3,2,0,1:T(8,128)(2,1)} %slice.496), channel_id=1, source_target_pairs={{0,16},{2,18},{4,20},{6,22},{8,24},{10,26},{12,28},{14,30},{16,0},... | collective-permute-start | bytes 393224 | tf_op jit(solution)/shard_map/ppermute | solution.py:485
  373.2 27.2 %collective-permute-start.40 = (bf16[2,64,2048]{2,1,0:T(8,128)(2,1)S(1)}, bf16[2,64,2048]{2,1,0:T(8,128)(2,1)S(1)}, u32[]{:S(2)}, u32[]{:S(2)}) collective-permute-start(bf16[2,64,2048]{2,1,0:T(8,128)(2,1)S(1)} %dynamic-slice_bitcast_fusion), channel_id=1, source_target_pairs={{0,8},{2,10},{4,12},{6,14},{8,0},{10,2},{12,4},{14,6},{16,24},{18,... | collective-permute-start | bytes 1572872 | tf_op jit(solution)/shard_map/ppermute | solution.py:485
  (84 other events, 530.5 us)
Sparse Core Ops, SparseCore 0:
  10.8 154.6 all-gather.1
  216.0 59.8 reduce-scatter.7
  279.1 82.7 reduce-scatter.3
  373.4 31.5 reduce-scatter.5
